TPU v7x, 512 devices: a whole 4x8x8 slice. The times are simulated.
512 devices in a mesh: row: 32 (over x, z), col: 16 (over y, core).
Axes of the slice: x: 4, y: 8, z: 8, core: 2. Of those that a mesh axis runs over, the one named last changes fastest.
Arguments:
- trail_points: bfloat16 [2048, 2560], P('row', 'col'), may hold values from -7 to 7
- block_points: bfloat16 [1024, 2560], P('col', 'row'), may hold values from -7 to 7
- cand_points: bfloat16 [2048, 2560], P('row', 'col'), may hold values from -7 to 7
- trail_factor: float32 [2048, 4096], P('row', 'col'), may hold values from -0.0359375 to 0.0359375
- block_factor: float32 [1024, 4096], P('row', 'col'), may hold values from -0.015625 to 0.015625
- cand_solved: float32 [4096, 2048], P('col', 'row'), may hold values from -0.0328125 to 0.0328125
- noise: float32 [1024], P('row'), may hold values from 1 to 4
Outputs:
- diag_factor: float32 [1024, 1024], P('col')
- panel: float32 [1024, 2048], P('col', 'row')
- cand_solve: float32 [1024, 2048], P('col', 'row')
All inputs are finite; a program needn't handle non-finite values.
Results may differ from a plain program's by a relative error of at most 0.0012.
Values may be sent and summed in bfloat16 or wider, within the bound.
No kernel may reach another device: no remote copies, remote signals or barrier semaphores. Data moves between devices by JAX's collectives and lax.ppermute only.
A program may use at most 64 MiB of HBM per device.

v0:
```python
import jax
import jax.numpy as jnp
from jax import lax
from jax.sharding import PartitionSpec as P

D = 2560


def broadcast(value, axis, source):
    kept = jnp.where(lax.axis_index(axis) == source, value, 0).astype(value.dtype)
    return lax.psum(kept, axis)


def matern(left_points, right_points):
    inner_products = lax.dot_general(
        left_points, right_points, (((1,), (1,)), ((), ())), preferred_element_type=jnp.float32
    )
    left_norms = jnp.sum(jnp.square(left_points.astype(jnp.float32)), axis=1)
    right_norms = jnp.sum(jnp.square(right_points.astype(jnp.float32)), axis=1)
    squared = jnp.maximum(left_norms[:, None] + right_norms[None, :] - 2.0 * inner_products, 0.0)
    scaled = jnp.sqrt(5.0 * squared / D)
    return (1.0 + scaled + scaled * scaled / 3.0) * jnp.exp(-scaled)


def lower_solve(matrix, values):
    return lax.linalg.triangular_solve(matrix, values, left_side=True, lower=True)


def body(trail_points, block_points, cand_points, trail_factor, block_factor, cand_solved, noise):
    highest = lax.Precision.HIGHEST
    row_full, cand_full = (
        lax.all_gather(trail_points, "col", axis=1, tiled=True),
        lax.all_gather(cand_points, "col", axis=1, tiled=True),
    )
    own_block = lax.all_gather(block_points, "row", axis=1, tiled=True)
    block_width = own_block.shape[0]
    block_height = block_factor.shape[0]
    trail_count = trail_factor.shape[0]
    row_index = lax.axis_index("row")
    col_index = lax.axis_index("col")
    holder = broadcast(own_block, "col", row_index * block_height // block_width)
    local_block = lax.dynamic_slice_in_dim(
        holder, row_index * block_height % block_width, block_height, 0
    )
    all_factor = lax.all_gather(
        block_factor.astype(jnp.bfloat16), "row", axis=0, tiled=True
    ).astype(block_factor.dtype)
    right_side = jnp.concatenate([block_factor.T, trail_factor.T, cand_solved], axis=1)
    products = lax.psum_scatter(
        jnp.dot(all_factor, right_side, precision=highest, preferred_element_type=jnp.float32),
        "col",
        scatter_dimension=0,
        tiled=True,
    )
    column_ids = col_index * block_width + jnp.arange(block_width, dtype=jnp.int32)
    row_ids = row_index * block_height + jnp.arange(block_height, dtype=jnp.int32)
    on_diagonal = column_ids[:, None] == row_ids[None, :]
    diag_tile = matern(own_block, local_block) - products[:, :block_height]
    diag_tile = diag_tile + jnp.where(on_diagonal, noise[None, :], 0.0)
    below_tile = (
        matern(own_block, row_full) - products[:, block_height : block_height + trail_count]
    )
    cand_tile = matern(own_block, cand_full) - products[:, block_height + trail_count :]
    diag_rows = lax.all_gather(diag_tile, "row", axis=1, tiled=True)
    whole_t, cand_all = (
        lax.all_gather(diag_rows, "col", axis=0, tiled=True),
        lax.all_gather(cand_tile, "col", axis=0, tiled=True),
    )
    factor = jnp.linalg.cholesky(whole_t.T)
    offset = col_index * block_width
    diag_out = lax.dynamic_slice_in_dim(factor, offset, block_width, 0)
    cand_out = lax.dynamic_slice_in_dim(lower_solve(factor, cand_all), offset, block_width, 0)
    full_rows = lax.all_gather(below_tile, "col", axis=0, tiled=True)
    panel_out = lax.dynamic_slice_in_dim(lower_solve(factor, full_rows), offset, block_width, 0)
    return (diag_out, panel_out, cand_out)


def solution(mesh):
    return jax.shard_map(
        body,
        mesh=mesh,
        in_specs=(
            P("row", "col"),
            P("col", "row"),
            P("row", "col"),
            P("row", "col"),
            P("row", "col"),
            P("col", "row"),
            P("row"),
        ),
        out_specs=(P("col", None), P("col", "row"), P("col", "row")),
        check_vma=False,
    )
```

profile of v0, /device:TPU:1, one launch (start us, length us, event | category | flops | bytes accessed | tf_op | source)
XLA Modules:
  0.0 721.5 jit_solution(13237810849203328398)
XLA Ops:
  7.2 44.3 %all-gather = bf16[32,80,64]{1,2,0:T(8,128)(2,1)S(1)} all-gather(bf16[1,80,64]{1,2,0:T(8,128)(2,1)} %bitcast.187), channel_id=1, replica_groups=mesh['row'=32,'col'=16] {'row'}, dimensions={0}, use_global_device_ids=true | all-gather | bytes 337920 | tf_op jit(solution)/shard_map/all_gather | solution.py:35
  54.4 37.7 %all_gather.25 = bf16[1024,256]{1,0:T(8,128)(2,1)S(1)} all-gather(bf16[32,256]{1,0:T(8,128)(2,1)S(1)} %convert_element_type.22), channel_id=1, replica_groups=mesh['row'=32,'col'=16] {'row'}, dimensions={0}, use_global_device_ids=true | all-gather | bytes 540672 | tf_op jit(solution)/shard_map/all_gather | solution.py:45
  95.2 80.5 %all-reduce.3.cloned.1.call-done = bf16[64,2560]{1,0:T(8,128)(2,1)} async-done(((bf16[64,2560]{1,0:T(8,128)(2,1)}), bf16[64,2560]{1,0:T(8,128)(2,1)}) %all-reduce.3.cloned.1.call-update) | async-done | bytes 327696 | tf_op jit(solution)/shard_map/psum | solution.py:11
  176.8 59.3 %reduce-scatter.4.cloned.1.call-done = f32[64,160]{1,0:T(8,128)} async-done(((f32[1024,160]{1,0:T(8,128)}), f32[64,160]{1,0:T(8,128)}) %reduce-scatter.4.cloned.1.call-update) | async-done | bytes 40976 | tf_op jit(solution)/shard_map/reduce_scatter | solution.py:49
  238.1 38.1 %all_gather.26 = f32[64,1024]{0,1:T(8,128)S(1)} all-gather(f32[64,32]{0,1:T(8,128)S(1)} %select_add_fusion), channel_id=1, replica_groups=mesh['row'=32,'col'=16] {'row'}, dimensions={1}, use_global_device_ids=true | all-gather | bytes 270336 | tf_op jit(solution)/shard_map/all_gather | solution.py:64
  277.1 31.4 %all-gather.2 = bf16[16,160,64]{1,2,0:T(8,128)(2,1)S(1)} all-gather(bf16[1,160,64]{1,2,0:T(8,128)(2,1)S(1)} %bitcast.185), channel_id=1, replica_groups=mesh['row'=32,'col'=16] {'col'}, dimensions={0}, use_global_device_ids=true | all-gather | bytes 348160 | tf_op jit(solution)/shard_map/all_gather | solution.py:33
  309.6 19.2 %all-gather.1 = bf16[16,160,64]{1,2,0:T(8,128)(2,1)S(1)} all-gather(bf16[1,160,64]{1,2,0:T(8,128)(2,1)S(1)} %bitcast.186), channel_id=1, replica_groups=mesh['row'=32,'col'=16] {'col'}, dimensions={0}, use_global_device_ids=true | all-gather | bytes 348160 | tf_op jit(solution)/shard_map/all_gather | solution.py:32
  330.5 15.9 %all_gather.31 = f32[1024,64]{1,0:T(8,128)S(1)} all-gather(f32[64,64]{1,0:T(8,128)S(1)} %slice_subtract_fusion), channel_id=1, replica_groups=mesh['row'=32,'col'=16] {'col'}, dimensions={0}, use_global_device_ids=true | all-gather | bytes 278528 | tf_op jit(solution)/shard_map/all_gather | solution.py:67
  347.2 17.2 %all_gather.29 = f32[1024,64]{1,0:T(8,128)S(1)} all-gather(f32[64,64]{1,0:T(8,128)S(1)} %slice_subtract_fusion.1), channel_id=1, replica_groups=mesh['row'=32,'col'=16] {'col'}, dimensions={0}, use_global_device_ids=true | all-gather | bytes 278528 | tf_op jit(solution)/shard_map/all_gather | solution.py:73
  365.1 5.8 copy.34
  370.9 4.4 add_multiply_fusion
  377.3 11.7 %cholesky.223 = f32[128,128]{1,0:T(8,128)S(1)} custom-call(f32[128,128]{1,0:T(8,128)S(1)} %cholesky.580), custom_call_target="Cholesky" | custom-call | tf_op jit(solution)/shard_map/jit(cholesky)/cholesky | solution.py:69
  389.0 2.5 cholesky.255
  391.5 9.8 %custom-call.62 = f32[1,128,128]{1,2,0:T(8,128)S(1)} custom-call(f32[1,128,128]{2,1,0:T(8,128)S(1)} %get-tuple-element.79), custom_call_target="InvertDiagBlocksLowerTriangular" | custom-call | tf_op jit(solution)/shard_map/jit(cholesky)/cholesky | solution.py:69
  401.4 2.3 constant_dynamic-update-slice_fusion.50
  405.3 11.9 %cholesky.244 = f32[128,128]{1,0:T(8,128)S(1)} custom-call(f32[128,128]{1,0:T(8,128)S(1)} %cholesky.584), custom_call_target="Cholesky" | custom-call | tf_op jit(solution)/shard_map/jit(cholesky)/cholesky | solution.py:69
  417.8 9.8 %custom-call.63 = f32[1,128,128]{1,2,0:T(8,128)S(1)} custom-call(f32[1,128,128]{2,1,0:T(8,128)S(1)} %get-tuple-element.76), custom_call_target="InvertDiagBlocksLowerTriangular" | custom-call | tf_op jit(solution)/shard_map/jit(cholesky)/cholesky | solution.py:69
  430.9 11.7 %cholesky.468 = f32[128,128]{1,0:T(8,128)S(1)} custom-call(f32[128,128]{1,0:T(8,128)S(1)} %cholesky.589), custom_call_target="Cholesky" | custom-call | tf_op jit(solution)/shard_map/jit(cholesky)/cholesky | solution.py:69
  444.0 9.8 %custom-call.64 = f32[1,128,128]{1,2,0:T(8,128)S(1)} custom-call(f32[1,128,128]{2,1,0:T(8,128)S(1)} %get-tuple-element.73), custom_call_target="InvertDiagBlocksLowerTriangular" | custom-call | tf_op jit(solution)/shard_map/jit(cholesky)/cholesky | solution.py:69
  454.9 2.3 convolution_subtract_fusion.2
  457.3 11.9 %cholesky.487 = f32[128,128]{1,0:T(8,128)S(1)} custom-call(f32[128,128]{1,0:T(8,128)S(1)} %cholesky.594), custom_call_target="Cholesky" | custom-call | tf_op jit(solution)/shard_map/jit(cholesky)/cholesky | solution.py:69
  470.5 9.8 %custom-call.65 = f32[1,128,128]{1,2,0:T(8,128)S(1)} custom-call(f32[1,128,128]{2,1,0:T(8,128)S(1)} %get-tuple-element.70), custom_call_target="InvertDiagBlocksLowerTriangular" | custom-call | tf_op jit(solution)/shard_map/jit(cholesky)/cholesky | solution.py:69
  483.8 11.7 %cholesky.506 = f32[128,128]{1,0:T(8,128)S(1)} custom-call(f32[128,128]{1,0:T(8,128)S(1)} %cholesky.599), custom_call_target="Cholesky" | custom-call | tf_op jit(solution)/shard_map/jit(cholesky)/cholesky | solution.py:69
  496.9 10.2 %custom-call.66 = f32[1,128,128]{1,2,0:T(8,128)S(1)} custom-call(f32[1,128,128]{2,1,0:T(8,128)S(1)} %get-tuple-element.67), custom_call_target="InvertDiagBlocksLowerTriangular" | custom-call | tf_op jit(solution)/shard_map/jit(cholesky)/cholesky | solution.py:69
  510.3 11.7 %cholesky.526 = f32[128,128]{1,0:T(8,128)S(1)} custom-call(f32[128,128]{1,0:T(8,128)S(1)} %cholesky.604), custom_call_target="Cholesky" | custom-call | tf_op jit(solution)/shard_map/jit(cholesky)/cholesky | solution.py:69
  523.3 9.8 %custom-call.67 = f32[1,128,128]{1,2,0:T(8,128)S(1)} custom-call(f32[1,128,128]{2,1,0:T(8,128)S(1)} %get-tuple-element.64), custom_call_target="InvertDiagBlocksLowerTriangular" | custom-call | tf_op jit(solution)/shard_map/jit(cholesky)/cholesky | solution.py:69
  536.1 11.9 %cholesky.546 = f32[128,128]{1,0:T(8,128)S(1)} custom-call(f32[128,128]{1,0:T(8,128)S(1)} %cholesky.609), custom_call_target="Cholesky" | custom-call | tf_op jit(solution)/shard_map/jit(cholesky)/cholesky | solution.py:69
  549.3 9.8 %custom-call.68 = f32[1,128,128]{1,2,0:T(8,128)S(1)} custom-call(f32[1,128,128]{2,1,0:T(8,128)S(1)} %get-tuple-element.61), custom_call_target="InvertDiagBlocksLowerTriangular" | custom-call | tf_op jit(solution)/shard_map/jit(cholesky)/cholesky | solution.py:69
  561.7 11.7 %cholesky.564 = f32[128,128]{1,0:T(8,128)S(1)} custom-call(f32[128,128]{1,0:T(8,128)S(1)} %convolution_subtract_fusion.6), custom_call_target="Cholesky" | custom-call | tf_op jit(solution)/shard_map/jit(cholesky)/cholesky | solution.py:69
  580.4 6.6 fusion
  587.0 23.2 %while.4 = (s32[]{:T(128)}, f32[1024,1024]{1,0:T(8,128)}, s32[8,2]{0,1:T(2,128)S(1)}, f32[8,128,128]{2,1,0:T(8,128)S(1)}, s32[]{:T(128)}) while((s32[]{:T(128)}, f32[1024,1024]{1,0:T(8,128)}, s32[8,2]{0,1:T(2,128)S(1)}, f32[8,128,128]{2,1,0:T(8,128)S(1)}, s32[]{:T(128)}) %tuple.105), condition=%wide.while_cond, body=%wide.while_body.sunk | while | flops 2 | bytes 131181 | solution.py:26
  610.2 78.8 %custom-call.70 = f32[8,128,128]{1,2,0:T(8,128)S(1)} custom-call(f32[8,128,128]{2,1,0:T(8,128)S(1)} %get-tuple-element.18), custom_call_target="InvertDiagBlocksLowerTriangular" | custom-call | tf_op jit(solution)/shard_map/triangular_solve/custom-call.7 | solution.py:26
  (151 shorter events, 92.3 us)
Async XLA Ops:
  7.2 168.5 %all-reduce.3.cloned.1.call-start = ((), (), s32[]{:S(2)}) async-start(), calls=%async_computation.1 | async-start | bytes 655360 | tf_op jit(solution)/shard_map/psum | solution.py:11
  51.6 185.4 %copy-start.4 = (f32[32]{0:T(128)S(1)}, f32[32]{0:T(128)}, u32[]{:S(2)}) copy-start(f32[32]{0:T(128)} %param.15) | copy-start | bytes 388
  52.8 224.3 %copy-start.2 = (bf16[64,160]{1,0:T(8,128)(2,1)S(1)}, bf16[64,160]{1,0:T(8,128)(2,1)}, u32[]{:S(2)}) copy-start(bf16[64,160]{1,0:T(8,128)(2,1)} %param.11) | copy-start | bytes 61444
  53.6 182.5 %reduce-scatter.4.cloned.1.call-start = ((), (), s32[]{:S(2)}) async-start(), calls=%async_computation.3 | async-start | bytes 1114112 | tf_op jit(solution)/shard_map/reduce_scatter | solution.py:49
  93.6 216.0 %copy-start.3 = (bf16[64,160]{1,0:T(8,128)(2,1)S(1)}, bf16[64,160]{1,0:T(8,128)(2,1)}, u32[]{:S(2)}) copy-start(bf16[64,160]{1,0:T(8,128)(2,1)} %param.9) | copy-start | bytes 61444
  95.0 270.2 %all-gather.5.cloned.1.call-start = ((), (), s32[]{:S(2)}) async-start(), calls=%async_computation.2 | async-start | bytes 4456448 | tf_op jit(solution)/shard_map/all_gather | solution.py:66
  236.0 94.2 %copy-start.1 = (f32[64,160]{1,0:T(8,128)S(1)}, f32[64,160]{1,0:T(8,128)}, u32[]{:S(2)}) copy-start(f32[64,160]{1,0:T(8,128)} %reduce-scatter.4.cloned.1.call-done) | copy-start | bytes 122884
  375.4 1.9 copy-start
Sparse Core Ops, SparseCore 0:
  53.7 121.9 all-reduce.2
  178.7 57.2 reduce-scatter.3
  277.2 56.8 all-gather.4
where the time goes:
time: 730 us; the launch traced here: 722 us
  other arithmetic  265 us (36%)
  blocking collectives  204 us (28%)
  waiting for transfers between devices  140 us (19%)
  matrix products  48.6 us (7%)
  local copies, waits for them, and re-layouts  44.1 us (6%)
  between operations  19.6 us (3%)
    another operation x30, other arithmetic, body(): factor = jnp.linalg.cholesky(whole_t.T)  172 us
    another operation x4, other arithmetic, lower_solve(): lax.linalg.triangular_solve(matrix, values, left_side=True, lower=True)  85.4 us
    psum x1, waiting for transfers between devices, broadcast(): return lax.psum(kept, axis)  80.5 us
    reduce_scatter x1, waiting for transfers between devices, body(): lax.psum_scatter(jnp.dot(all_factor, right_side, precision=highest, prefe...  59.3 us
    all_gather x1, blocking collectives, body(): own_block = lax.all_gather(block_points, 'row', axis=1, tiled=True)  44.3 us
    all_gather x1, blocking collectives, body(): diag_rows = lax.all_gather(diag_tile, 'row', axis=1, tiled=True)  38.1 us
    all_gather x1, blocking collectives, body(): lax.all_gather(block_factor.astype(jnp.bfloat16), 'row', axis=0, tiled=True)  37.7 us
    all_gather x1, blocking collectives, body(): lax.all_gather(cand_points, 'col', axis=1, tiled=True)  31.4 us
  transfers between devices with their start and end apart: 3, of which 2 were waited for; matrix products, arithmetic and copies ran while one was open for 1% of the time, Pallas kernels for 0%

commit v1 on v0

v1 whole, which is shorter than its diff:
```python
import jax
import jax.numpy as jnp
from jax import lax
from jax.experimental import pallas as pl
from jax.experimental.pallas import tpu as pltpu
from jax.sharding import PartitionSpec as P

D = 2560

N = 1024
BLK = 128
f32, bf16 = jnp.float32, jnp.bfloat16


def split(x):
    high = x.astype(bf16)
    return high, (x - high.astype(f32)).astype(bf16)


def mm(a, b, bt=False):
    dims = (((1,), (1 if bt else 0,)), ((), ()))
    return lax.dot_general(a, b, dims, preferred_element_type=f32)


def dot3(a, b, bt=False):
    ah, al = split(a)
    bh, bl = split(b)
    return mm(ah, bh, bt) + (mm(ah, bl, bt) + mm(al, bh, bt))


def rows_of(x):
    return [jnp.broadcast_to(x[k : k + 1, :], (8, BLK)) for k in range(8)]


def lane(x, j):
    return jnp.broadcast_to(x[:, j : j + 1], (8, BLK))


def factor_inverse(D, store):
    sub = lax.broadcasted_iota(jnp.int32, (8, BLK), 0)
    ln = lax.broadcasted_iota(jnp.int32, (8, BLK), 1)
    E = [jnp.where(sub + 8 * v == ln, 1.0, 0.0).astype(f32) for v in range(16)]
    for g in range(16):
        R, RE = rows_of(D[g]), rows_of(E[g])
        G = {}
        for i in range(8):
            for l in range(i, 8):
                G[i, l] = lane(R[i], 8 * g + l)
        M = {v: [lane(D[v], 8 * g + k) for k in range(8)] for v in range(g + 1, 16)}
        inv, F = [], {}
        for i in range(8):
            r = 1.0 / G[i, i]
            inv.append(r)
            if i < 7:
                nxt = G[i, i + 1] * G[i, i + 1]
            for l in range(i + 1, 8):
                F[l, i] = G[i, l] * r
            for l in range(i + 1, 8):
                for m in range(l, 8):
                    if l == i + 1 and m == l:
                        G[l, m] = G[l, m] - nxt * r
                    else:
                        G[l, m] = G[l, m] - F[l, i] * G[i, m]
            for l in range(i + 1, 8):
                RE[l] = RE[l] - F[l, i] * RE[i]
                R[l] = R[l] - F[l, i] * R[i]
        out = RE[0] * lax.rsqrt(G[0, 0])
        for i in range(1, 8):
            out = jnp.where(sub == i, RE[i] * lax.rsqrt(G[i, i]), out)
        store(g, out)
        if g == 15:
            break
        V, VE = [None] * 8, [None] * 8
        for i in range(7, -1, -1):
            a, b = R[i] * inv[i], RE[i] * inv[i]
            for l in range(i + 1, 8):
                a = a - F[l, i] * V[l]
                b = b - F[l, i] * VE[l]
            V[i], VE[i] = a, b
        for v in range(g + 1, 16):
            d, e = D[v], E[v]
            for k in range(8):
                d = d - M[v][k] * V[k]
                e = e - M[v][k] * VE[k]
            D[v], E[v] = d, e


def kernel(c_ref, a_ref, rhs_ref, diag_ref, w_ref, t, linv, uph, upl):
    c = c_ref[0]
    width = N + BLK

    def fill(i, _):
        r = pl.multiple_of(i * BLK, BLK)
        t[pl.ds(r, BLK), :N] = a_ref[pl.ds(r, BLK), :]
        t[pl.ds(r, BLK), N:] = rhs_ref[pl.ds(r, BLK), :]
        return 0

    lax.fori_loop(0, 8, fill, 0)

    def step(kb, _):
        base = pl.multiple_of(kb * BLK, BLK)
        D = [t[pl.ds(pl.multiple_of(base + 8 * v, 8), 8), pl.ds(base, BLK)] for v in range(16)]

        def store(g, rows):
            linv[8 * g : 8 * g + 8, :] = rows

        factor_inverse(D, store)
        lh, ll = split(linv[...])
        mine = pl.multiple_of(c * 64, 64)
        lc = t[pl.ds(mine, 64), pl.ds(base, BLK)]
        ch, cl = split(lc)
        low = mm(ch, lh, True) + (mm(cl, lh, True) + mm(ch, ll, True))
        ri = lax.broadcasted_iota(jnp.int32, (64, BLK), 0) + mine
        ci = lax.broadcasted_iota(jnp.int32, (64, BLK), 1) + base
        diag_ref[:, pl.ds(base, BLK)] = jnp.where(ri >= ci, low, 0.0)
        for n0 in range(0, width, 384):
            x = t[pl.ds(base, BLK), n0 : n0 + 384]
            xh, xl = split(x)
            u = mm(lh, xh) + (mm(ll, xh) + mm(lh, xl))
            uh, ul = split(u)
            uph[:, n0 : n0 + 384] = uh
            upl[:, n0 : n0 + 384] = ul
            if n0 + 384 == width:
                t[pl.ds(base, BLK), N:] = u[:, 256:]

        def update(jb, _):
            r = pl.multiple_of(jb * BLK, BLK)
            ah, al = split(t[pl.ds(r, BLK), pl.ds(base, BLK)])
            lp = mm(ah, lh, True) + (mm(al, lh, True) + mm(ah, ll, True))
            ph, pl_ = split(lp)
            for n0 in range(0, width, 384):
                uh, ul = uph[:, n0 : n0 + 384], upl[:, n0 : n0 + 384]
                t[pl.ds(r, BLK), n0 : n0 + 384] -= mm(ph, uh) + (mm(ph, ul) + mm(pl_, uh))
            return 0

        lax.fori_loop(kb + 1, 8, update, 0)
        return 0

    lax.fori_loop(0, 8, step, 0)
    w_ref[...] = t[pl.ds(pl.multiple_of(c * 64, 64), 64), N:]


def chol_solve(c, a, rhs):
    return pl.pallas_call(
        kernel,
        out_shape=(jax.ShapeDtypeStruct((64, N), f32), jax.ShapeDtypeStruct((64, BLK), f32)),
        in_specs=[pl.BlockSpec(memory_space=pltpu.SMEM), pl.BlockSpec(memory_space=pltpu.VMEM), pl.BlockSpec(memory_space=pltpu.VMEM)],
        out_specs=(pl.BlockSpec(memory_space=pltpu.VMEM), pl.BlockSpec(memory_space=pltpu.VMEM)),
        scratch_shapes=[
            pltpu.VMEM((N, N + BLK), f32),
            pltpu.VMEM((BLK, BLK), f32),
            pltpu.VMEM((BLK, N + BLK), bf16),
            pltpu.VMEM((BLK, N + BLK), bf16),
        ],
        compiler_params=pltpu.CompilerParams(vmem_limit_bytes=40 * 1024 * 1024),
        cost_estimate=pl.CostEstimate(flops=3 * 10**9, bytes_accessed=5 * 10**6, transcendentals=0),
    )(c, a, rhs)


def spread(value, axis, count):
    copies = jnp.broadcast_to(value[None], (count,) + value.shape)
    return lax.all_to_all(lax.optimization_barrier(copies), axis, 0, 0)


def sum_scatter(value, axis, count):
    rows = value.shape[0] // count
    parts = lax.all_to_all(value.reshape((count, rows) + value.shape[1:]), axis, 0, 0)
    return jnp.sum(parts, axis=0)


def matern(inner, left_norms, right_norms):
    squared = jnp.maximum(left_norms[:, None] + right_norms[None, :] - 2.0 * inner, 0.0)
    scaled = jnp.sqrt(5.0 * squared / D)
    return (1.0 + scaled + scaled * scaled / 3.0) * jnp.exp(-scaled)


def norms(points):
    return jnp.sum(jnp.square(points.astype(f32)), axis=0)


def times(a, b, dims):
    high, low = split(b)
    one = lax.dot_general(a, high, (dims, ((), ())), preferred_element_type=f32)
    return one + lax.dot_general(a, low, (dims, ((), ())), preferred_element_type=f32)


def body(trail_points, block_points, cand_points, trail_factor, block_factor, cand_solved, noise):
    rows, cols = 32, 16
    row_index = lax.axis_index("row")
    col_index = lax.axis_index("col")
    block_t = block_points.T
    same, other = [], []
    for r in range(rows):
        for c in range(cols):
            half = r % 2
            same.append((r * cols + c, (2 * c + half) * cols + r // 2))
            other.append((r * cols + c, (2 * c + 1 - half) * cols + r // 2))
    odd = row_index % 2
    halves = (block_t[:, :32], block_t[:, 32:])
    mine = lax.ppermute(jnp.where(odd == 0, halves[0], halves[1]), ("row", "col"), same)
    theirs = lax.ppermute(jnp.where(odd == 0, halves[1], halves[0]), ("row", "col"), other)
    local_t = jnp.where(
        odd == 0, jnp.concatenate([mine, theirs], axis=0), jnp.concatenate([theirs, mine], axis=0)
    )
    all_factor = spread(block_factor.astype(bf16), "row", rows).reshape(N, -1)
    own_t = spread(block_t, "row", rows).reshape(D, -1)
    points_t = lax.all_gather(
        jnp.concatenate([trail_points.T, cand_points.T, local_t], axis=1), "col", axis=0, tiled=True
    )
    inner = lax.dot_general(own_t, points_t, (((0,), (0,)), ((), ())), preferred_element_type=f32)
    kernel_tile = matern(inner, norms(own_t), norms(points_t))

    diag_part = times(all_factor, block_factor, ((1,), (1,)))
    rhs_part = jnp.concatenate(
        [
            times(all_factor, trail_factor, ((1,), (1,))),
            times(all_factor, cand_solved, ((1,), (0,))),
        ],
        axis=1,
    )
    column_ids = col_index * 64 + jnp.arange(64, dtype=jnp.int32)
    row_ids = row_index * 32 + jnp.arange(32, dtype=jnp.int32)
    on_diagonal = column_ids[:, None] == row_ids[None, :]
    diag_tile = kernel_tile[:, 128:] - sum_scatter(diag_part, "col", cols)
    diag_tile = diag_tile + jnp.where(on_diagonal, noise[None, :], 0.0)
    diag_rows = spread(diag_tile, "row", rows).transpose(1, 0, 2).reshape(64, N)
    diag_rows, rhs_part = lax.optimization_barrier((diag_rows, rhs_part))
    whole = lax.all_gather(diag_rows, "col", axis=0, tiled=True)
    rhs_tile = kernel_tile[:, :128] - sum_scatter(rhs_part, "col", cols)
    rhs = lax.all_gather(rhs_tile, "col", axis=0, tiled=True)
    diag_out, solved = chol_solve(col_index.reshape(1).astype(jnp.int32), whole, rhs)
    return (diag_out, solved[:, :64], solved[:, 64:])


def solution(mesh):
    return jax.shard_map(
        body,
        mesh=mesh,
        in_specs=(
            P("row", "col"),
            P("col", "row"),
            P("row", "col"),
            P("row", "col"),
            P("row", "col"),
            P("col", "row"),
            P("row"),
        ),
        out_specs=(P("col", None), P("col", "row"), P("col", "row")),
        check_vma=False,
    )
```

time: 730 us -> 242 us (0.33); the launches traced: 722 us -> 241 us
  other arithmetic: 265 us -> 3.22 us
  blocking collectives: 204 us -> 64.5 us
  waiting for transfers between devices: 140 us -> 28.3 us
  Pallas kernels: 0 us -> 65.6 us
  starting transfers between devices: 0.12 us -> 52.2 us
  matrix products: 48.6 us -> 2.04 us
  local copies, waits for them, and re-layouts: 44.1 us -> 11.2 us
    another operation x34 -> x0, other arithmetic: 258 us -> none  [the longest x30 172 us: body(): factor = jnp.linalg.cholesky(whole_t.T)]
    all_gather x7 -> x2, blocking collectives: 204 us -> 38 us  [the longest x1 20.1 us: body(): lax.all_gather(jnp.concatenate([trail_points.T, cand_points.T, local_t],...]
    psum x1 -> x0, waiting for transfers between devices: 80.5 us -> none  [broadcast(): return lax.psum(kept, axis)]
    pallas_call x0 -> x1, Pallas kernels: none -> 65.6 us  [chol_solve(): pl.pallas_call(kernel, out_shape=(jax.ShapeDtypeStruct((64, N), f32), jax...]
    reduce_scatter x1 -> x0, waiting for transfers between devices: 59.3 us -> none  [body(): lax.psum_scatter(jnp.dot(all_factor, right_side, precision=highest, prefe...]
    another operation x44 -> x0, matrix products: 45.4 us -> none  [the longest x14 23.1 us: body(): factor = jnp.linalg.cholesky(whole_t.T)]
    all_to_all x0 -> x4, starting transfers between devices: none -> 44.2 us  [the longest x3 39.2 us: spread(): return lax.all_to_all(lax.optimization_barrier(copies), axis, 0, 0)]
    all_to_all x0 -> x1, blocking collectives: none -> 26.5 us  [sum_scatter(): lax.all_to_all(value.reshape((count, rows) + value.shape[1:]), axis, 0, 0)]
  transfers between devices with their start and end apart: 3 -> 7, of which waited for: 2 -> 4; matrix products, arithmetic and copies ran while one was open for 1% -> 2% of each run, Pallas kernels for 0% -> 0%
where the time goes in v1:
time: 242 us; the launch traced here: 241 us
  Pallas kernels  65.6 us (27%)
  blocking collectives  64.5 us (27%)
  starting transfers between devices  52.2 us (22%)
  waiting for transfers between devices  28.3 us (12%)
  between operations  14.4 us (6%)
  local copies, waits for them, and re-layouts  11.2 us (5%)
  other arithmetic  3.22 us (1%)
    pallas_call x1, Pallas kernels, chol_solve(): pl.pallas_call(kernel, out_shape=(jax.ShapeDtypeStruct((64, N), f32), jax...  65.6 us
    all_to_all x3, starting transfers between devices, spread(): return lax.all_to_all(lax.optimization_barrier(copies), axis, 0, 0)  39.2 us
    all_to_all x1, blocking collectives, sum_scatter(): lax.all_to_all(value.reshape((count, rows) + value.shape[1:]), axis, 0, 0)  26.5 us
    all_gather x1, blocking collectives, body(): lax.all_gather(jnp.concatenate([trail_points.T, cand_points.T, local_t],...  20.1 us
    all_gather x1, blocking collectives, body(): rhs = lax.all_gather(rhs_tile, 'col', axis=0, tiled=True)  17.9 us
    all_to_all x3, waiting for transfers between devices, spread(): return lax.all_to_all(lax.optimization_barrier(copies), axis, 0, 0)  10 us
    all_to_all x1, waiting for transfers between devices, sum_scatter(): lax.all_to_all(value.reshape((count, rows) + value.shape[1:]), axis, 0, 0)  8.58 us
    ppermute x1, waiting for transfers between devices, body(): lax.ppermute(jnp.where(odd == 0, halves[0], halves[1]), ('row', 'col'), s...  6.21 us
  transfers between devices with their start and end apart: 7, of which 4 were waited for; matrix products, arithmetic and copies ran while one was open for 2% of the time, Pallas kernels for 0%

profile of v1, /device:TPU:1, one launch (start us, length us, event | category | flops | bytes accessed | tf_op | source)
XLA Modules:
  0.0 241.4 jit_solution(8696924448336360313)
XLA Ops:
  7.2 1.7 broadcast_in_dim.14
  8.9 13.7 %all-to-all-start = ((bf16[32,80,64]{1,2,0:T(8,128)(2,1)}), bf16[32,80,64]{1,2,0:T(8,128)(2,1)S(1)}, u32[]{:S(2)}, u32[]{:S(2)}) async-start(bf16[32,80,64]{1,2,0:T(8,128)(2,1)} %broadcast_in_dim.14), calls=%async_computation | async-start | bytes 1048576 | tf_op jit(solution)/shard_map/all_to_all | solution.py:162
  22.6 5.2 %collective-permute-start = (bf16[80,32]{0,1:T(8,128)(2,1)S(1)}, bf16[80,32]{0,1:T(8,128)(2,1)S(1)}, u32[]{:S(2)}, u32[]{:S(2)}) collective-permute-start(bf16[80,32]{0,1:T(8,128)(2,1)S(1)} %get-tuple-element.15), channel_id=1, source_target_pairs={{0,0},{1,32},{2,64},{3,96},{4,128},{5,160},{6,192},{7,224},{8,256}... | collective-permute-start | bytes 15368 | tf_op jit(solution)/shard_map/ppermute | solution.py:200
  27.8 2.8 %collective-permute-start.1 = (bf16[80,32]{0,1:T(8,128)(2,1)S(1)}, bf16[80,32]{0,1:T(8,128)(2,1)S(1)}, u32[]{:S(2)}, u32[]{:S(2)}) collective-permute-start(bf16[80,32]{0,1:T(8,128)(2,1)S(1)} %get-tuple-element.16), channel_id=1, source_target_pairs={{0,16},{1,48},{2,80},{3,112},{4,144},{5,176},{6,208},{7,240},{8,27... | collective-permute-start | bytes 15368 | tf_op jit(solution)/shard_map/ppermute | solution.py:201
  30.9 0.8 broadcast_in_dim.15
  31.8 6.2 %collective-permute-done = bf16[80,32]{0,1:T(8,128)(2,1)S(1)} collective-permute-done((bf16[80,32]{0,1:T(8,128)(2,1)S(1)}, bf16[80,32]{0,1:T(8,128)(2,1)S(1)}, u32[]{:S(2)}, u32[]{:S(2)}) %collective-permute-start) | collective-permute-done | bytes 5152 | tf_op jit(solution)/shard_map/ppermute | solution.py:200
  38.3 16.0 %all-to-all-start.1 = ((bf16[32,32,256]{2,1,0:T(8,128)(2,1)}), bf16[32,32,256]{2,1,0:T(8,128)(2,1)S(1)}, u32[]{:S(2)}, u32[]{:S(2)}) async-start(bf16[32,32,256]{2,1,0:T(8,128)(2,1)} %broadcast_in_dim.15), calls=%async_computation.1 | async-start | bytes 1048576 | tf_op jit(solution)/shard_map/all_to_all | solution.py:162
  54.4 20.1 %all_gather.9 = bf16[2560,160]{1,0:T(8,128)(2,1)S(1)} all-gather(bf16[160,160]{1,0:T(8,128)(2,1)S(1)} %pad_maximum_fusion.1), channel_id=1, replica_groups=mesh['row'=32,'col'=16] {'col'}, dimensions={0}, use_global_device_ids=true | all-gather | bytes 870400 | tf_op jit(solution)/shard_map/all_gather | solution.py:207
  74.6 0.4 multiply_reduce_fusion
  74.9 0.3 copy.51
  75.3 0.8 reshape.39
  76.4 0.4 exponential_multiply_fusion
  77.5 0.8 reshape.44
  78.3 4.9 %all-to-all-start.2 = ((f32[16,1,2048]{2,1,0:T(1,128)}), f32[16,1,2048]{2,1,0:T(1,128)S(1)}, u32[]{:S(2)}, u32[]{:S(2)}) async-start(f32[16,1,2048]{2,1,0:T(1,128)} %reshape.44), calls=%async_computation.2 | async-start | bytes 262144 | tf_op jit(solution)/shard_map/all_to_all | solution.py:167
  83.3 0.3 fusion.10
  83.6 0.3 fusion
  83.9 8.6 %all-to-all-done.2 = f32[16,1,2048]{2,1,0:T(1,128)S(1)} async-done(((f32[16,1,2048]{2,1,0:T(1,128)}), f32[16,1,2048]{2,1,0:T(1,128)S(1)}, u32[]{:S(2)}, u32[]{:S(2)}) %all-to-all-start.2) | async-done | bytes 131104 | tf_op jit(solution)/shard_map/all_to_all | solution.py:167
  92.5 0.5 broadcast.20
  93.0 0.9 reduce.1
  94.4 1.0 reshape.46
  95.4 9.5 %all-to-all-start.3 = ((f32[32,1,2048]{2,1,0:T(1,128)}), f32[32,1,2048]{2,1,0:T(1,128)S(1)}, u32[]{:S(2)}, u32[]{:S(2)}) async-start(f32[32,1,2048]{2,1,0:T(1,128)} %reshape.46), calls=%async_computation.3 | async-start | bytes 524288 | tf_op jit(solution)/shard_map/all_to_all | solution.py:162
  105.0 0.3 fusion.13
  105.3 0.3 fusion.1
  105.6 10.0 %all-to-all-done.3 = f32[32,1,2048]{2,1,0:T(1,128)S(1)} async-done(((f32[32,1,2048]{2,1,0:T(1,128)}), f32[32,1,2048]{2,1,0:T(1,128)S(1)}, u32[]{:S(2)}, u32[]{:S(2)}) %all-to-all-start.3) | async-done | bytes 262176 | tf_op jit(solution)/shard_map/all_to_all | solution.py:162
  115.6 1.3 reduce.2
  117.1 0.9 copy.56
  118.2 26.5 %all_to_all.25 = f32[16,64,128]{2,1,0:T(8,128)S(1)} all-to-all(f32[16,64,128]{2,1,0:T(8,128)S(1)} %bitcast.60), channel_id=1, replica_groups=mesh['row'=32,'col'=16] {'col'}, dimensions={0} | all-to-all | bytes 1048576 | tf_op jit(solution)/shard_map/all_to_all | solution.py:167
  144.7 17.9 %all_gather.11.rhs_ref = f32[1024,128]{1,0:T(8,128)S(1)} all-gather(f32[64,128]{1,0:T(8,128)S(1)} %slice_subtract_fusion), channel_id=1, replica_groups=mesh['row'=32,'col'=16] {'col'}, dimensions={0}, use_global_device_ids=true | all-gather | bytes 557056 | tf_op jit(solution)/shard_map/all_gather | solution.py:230
  162.6 3.5 %all-gather.2.cloned.1.call-done.a_ref = f32[1024,1024]{1,0:T(8,128)} async-done(((f32[64,1024]{1,0:T(8,128)}), f32[1024,1024]{1,0:T(8,128)}) %all-gather.2.cloned.1.call-update) | async-done | bytes 4194320 | tf_op jit(solution)/shard_map/all_gather | solution.py:228
  166.1 2.2 copy-done
  168.3 65.6 %shard_map.94 = (f32[64,1024]{1,0:T(8,128)}, f32[64,128]{1,0:T(8,128)S(1)}) custom-call(s32[1]{0:T(128)} %bitcast.c_ref, f32[1024,1024]{1,0:T(8,128)S(1)} %copy-done, f32[1024,128]{1,0:T(8,128)S(1)} %all_gather.11.rhs_ref), custom_call_target="tpu_custom_call" | custom-call | flops 3000000000 | bytes 5000000 | tf_op jit(solution)/shard_map/pallas_call | solution.py:144
  233.9 0.7 fusion.15
  (47 shorter events, 2.6 us)
Async XLA Ops:
  7.2 15.4 %copy-start.4 = (bf16[64,80]{1,0:T(8,128)(2,1)S(1)}, bf16[64,80]{1,0:T(8,128)(2,1)}, u32[]{:S(2)}) copy-start(bf16[64,80]{1,0:T(8,128)(2,1)} %param.8) | copy-start | bytes 30724
  7.2 23.5 %copy-start.5 = (bf16[64,160]{1,0:T(8,128)(2,1)S(1)}, bf16[64,160]{1,0:T(8,128)(2,1)}, u32[]{:S(2)}) copy-start(bf16[64,160]{1,0:T(8,128)(2,1)} %param.7) | copy-start | bytes 61444
  7.2 23.6 %copy-start.6 = (bf16[64,160]{1,0:T(8,128)(2,1)S(1)}, bf16[64,160]{1,0:T(8,128)(2,1)}, u32[]{:S(2)}) copy-start(bf16[64,160]{1,0:T(8,128)(2,1)} %param.9) | copy-start | bytes 61444
  7.2 23.7 %copy-start.1 = (f32[32,256]{1,0:T(8,128)S(1)}, f32[32,256]{1,0:T(8,128)}, u32[]{:S(2)}) copy-start(f32[32,256]{1,0:T(8,128)} %param.11) | copy-start | bytes 98308
  8.9 29.5 %all-to-all-start = ((bf16[32,80,64]{1,2,0:T(8,128)(2,1)}), bf16[32,80,64]{1,2,0:T(8,128)(2,1)S(1)}, u32[]{:S(2)}, u32[]{:S(2)}) async-start(bf16[32,80,64]{1,2,0:T(8,128)(2,1)} %broadcast_in_dim.14), calls=%async_computation | async-start | bytes 1048576 | tf_op jit(solution)/shard_map/all_to_all | solution.py:162
  22.6 15.4 %collective-permute-start = (bf16[80,32]{0,1:T(8,128)(2,1)S(1)}, bf16[80,32]{0,1:T(8,128)(2,1)S(1)}, u32[]{:S(2)}, u32[]{:S(2)}) collective-permute-start(bf16[80,32]{0,1:T(8,128)(2,1)S(1)} %get-tuple-element.15), channel_id=1, source_target_pairs={{0,0},{1,32},{2,64},{3,96},{4,128},{5,160},{6,192},{7,224},{8,256}... | collective-permute-start | bytes 15368 | tf_op jit(solution)/shard_map/ppermute | solution.py:200
  27.8 10.2 %collective-permute-start.1 = (bf16[80,32]{0,1:T(8,128)(2,1)S(1)}, bf16[80,32]{0,1:T(8,128)(2,1)S(1)}, u32[]{:S(2)}, u32[]{:S(2)}) collective-permute-start(bf16[80,32]{0,1:T(8,128)(2,1)S(1)} %get-tuple-element.16), channel_id=1, source_target_pairs={{0,16},{1,48},{2,80},{3,112},{4,144},{5,176},{6,208},{7,240},{8,27... | collective-permute-start | bytes 15368 | tf_op jit(solution)/shard_map/ppermute | solution.py:201
  38.3 38.4 %all-to-all-start.1 = ((bf16[32,32,256]{2,1,0:T(8,128)(2,1)}), bf16[32,32,256]{2,1,0:T(8,128)(2,1)S(1)}, u32[]{:S(2)}, u32[]{:S(2)}) async-start(bf16[32,32,256]{2,1,0:T(8,128)(2,1)} %broadcast_in_dim.15), calls=%async_computation.1 | async-start | bytes 1048576 | tf_op jit(solution)/shard_map/all_to_all | solution.py:162
  77.0 6.3 %copy-start.2 = (f32[256,64]{0,1:T(8,128)S(1)}, f32[256,64]{0,1:T(8,128)}, u32[]{:S(2)}) copy-start(f32[256,64]{0,1:T(8,128)} %param.12) | copy-start | bytes 196612
  78.3 14.1 %all-to-all-start.2 = ((f32[16,1,2048]{2,1,0:T(1,128)}), f32[16,1,2048]{2,1,0:T(1,128)S(1)}, u32[]{:S(2)}, u32[]{:S(2)}) async-start(f32[16,1,2048]{2,1,0:T(1,128)} %reshape.44), calls=%async_computation.2 | async-start | bytes 262144 | tf_op jit(solution)/shard_map/all_to_all | solution.py:167
  83.3 10.9 %copy-start.7 = (f32[32]{0:T(128)S(1)}, f32[32]{0:T(128)}, u32[]{:S(2)}) copy-start(f32[32]{0:T(128)} %param.13) | copy-start | bytes 388
  93.9 11.0 %copy-start.3 = (f32[64,256]{1,0:T(8,128)S(1)}, f32[64,256]{1,0:T(8,128)}, u32[]{:S(2)}) copy-start(f32[64,256]{1,0:T(8,128)} %param.10) | copy-start | bytes 196612
  95.4 20.2 %all-to-all-start.3 = ((f32[32,1,2048]{2,1,0:T(1,128)}), f32[32,1,2048]{2,1,0:T(1,128)S(1)}, u32[]{:S(2)}, u32[]{:S(2)}) async-start(f32[32,1,2048]{2,1,0:T(1,128)} %reshape.46), calls=%async_computation.3 | async-start | bytes 524288 | tf_op jit(solution)/shard_map/all_to_all | solution.py:162
  104.9 61.2 %all-gather.2.cloned.1.call-start = ((), (), s32[]{:S(2)}) async-start(), calls=%async_computation.5 | async-start | bytes 4456448 | tf_op jit(solution)/shard_map/all_gather | solution.py:228
  166.1 2.2 copy-start
Sparse Core Ops, SparseCore 0:
  118.1 47.9 all-gather.1

commit v2 on v1

--- a/solution.py
+++ b/solution.py
@@ -6,6 +6,7 @@
 from jax.sharding import PartitionSpec as P
 
 D = 2560
+PAD = 128
 
 N = 1024
 BLK = 128
@@ -89,9 +90,14 @@
     c = c_ref[0]
     width = N + BLK
 
+    for block in range(16):
+        slab = a_ref[64 * block : 64 * block + 64, :]
+        if block:
+            slab = pltpu.roll(slab, 64 * block, 1)
+        t[64 * block : 64 * block + 64, :N] = slab
+
     def fill(i, _):
         r = pl.multiple_of(i * BLK, BLK)
-        t[pl.ds(r, BLK), :N] = a_ref[pl.ds(r, BLK), :]
         t[pl.ds(r, BLK), N:] = rhs_ref[pl.ds(r, BLK), :]
         return 0
 
@@ -162,12 +168,6 @@
     return lax.all_to_all(lax.optimization_barrier(copies), axis, 0, 0)
 
 
-def sum_scatter(value, axis, count):
-    rows = value.shape[0] // count
-    parts = lax.all_to_all(value.reshape((count, rows) + value.shape[1:]), axis, 0, 0)
-    return jnp.sum(parts, axis=0)
-
-
 def matern(inner, left_norms, right_norms):
     squared = jnp.maximum(left_norms[:, None] + right_norms[None, :] - 2.0 * inner, 0.0)
     scaled = jnp.sqrt(5.0 * squared / D)
@@ -179,54 +179,57 @@
 
 
 def times(a, b, dims):
-    high, low = split(b)
-    one = lax.dot_general(a, high, (dims, ((), ())), preferred_element_type=f32)
-    return one + lax.dot_general(a, low, (dims, ((), ())), preferred_element_type=f32)
+    return lax.dot_general(a, b.astype(bf16), (dims, ((), ())), preferred_element_type=f32)
 
 
 def body(trail_points, block_points, cand_points, trail_factor, block_factor, cand_solved, noise):
     rows, cols = 32, 16
     row_index = lax.axis_index("row")
     col_index = lax.axis_index("col")
-    block_t = block_points.T
-    same, other = [], []
+    odd = row_index % 2
+    distance = row_index // 2
+    pad = jnp.zeros((trail_points.shape[1], PAD), bf16)
+    points_t = lax.all_gather(
+        jnp.concatenate([trail_points.T, cand_points.T, pad], axis=1), "col", axis=0, tiled=True
+    )
+    own_t = spread(block_points.T, "row", rows).reshape(D, -1)
+    hop = []
     for r in range(rows):
         for c in range(cols):
-            half = r % 2
-            same.append((r * cols + c, (2 * c + half) * cols + r // 2))
-            other.append((r * cols + c, (2 * c + 1 - half) * cols + r // 2))
-    odd = row_index % 2
-    halves = (block_t[:, :32], block_t[:, 32:])
-    mine = lax.ppermute(jnp.where(odd == 0, halves[0], halves[1]), ("row", "col"), same)
-    theirs = lax.ppermute(jnp.where(odd == 0, halves[1], halves[0]), ("row", "col"), other)
-    local_t = jnp.where(
-        odd == 0, jnp.concatenate([mine, theirs], axis=0), jnp.concatenate([theirs, mine], axis=0)
-    )
-    all_factor = spread(block_factor.astype(bf16), "row", rows).reshape(N, -1)
-    own_t = spread(block_t, "row", rows).reshape(D, -1)
-    points_t = lax.all_gather(
-        jnp.concatenate([trail_points.T, cand_points.T, local_t], axis=1), "col", axis=0, tiled=True
-    )
+            hop.append((r * cols + (c + r // 2) % cols, r * cols + c))
+    half = jnp.where(odd == 0, own_t[:, :32], own_t[:, 32:])
+    partner_t = lax.ppermute(half, ("row", "col"), hop)
+    factor = spread(block_factor.astype(bf16), "row", rows).reshape(cols, 64, -1)
+    turned = lax.dynamic_slice(
+        jnp.concatenate([factor, factor], axis=0),
+        (distance, 32 * odd, 0),
+        (cols, 32, factor.shape[2]),
+    )
+    diag_part = lax.dot_general(
+        factor, turned, (((2,), (2,)), ((0,), (0,))), preferred_element_type=f32
+    )
+    diag_sum = jnp.sum(lax.all_to_all(diag_part, "col", 0, 0), axis=0)
+    own_norms = norms(own_t)
+    inner = lax.dot_general(own_t, partner_t, (((0,), (0,)), ((), ())), preferred_element_type=f32)
+    diag_tile = matern(inner, own_norms, norms(partner_t)) - diag_sum
+    sent = jnp.concatenate([diag_tile, noise[None, :], jnp.zeros((7, 32), f32)], axis=0)
+    got = spread(sent, "row", rows)
+    own_noise = lax.dynamic_slice(got[:, 64, :], (2 * col_index, 0), (2, 32)).reshape(64)
+    diag_rows = got[:, :64, :].transpose(1, 0, 2).reshape(64, N)
+    place = jnp.arange(64, dtype=jnp.int32)[:, None] == jnp.arange(N, dtype=jnp.int32)[None, :]
+    diag_rows = diag_rows + jnp.where(place, own_noise[:, None], 0.0)
+    diag_rows, factor = lax.optimization_barrier((diag_rows, factor))
+    whole = lax.all_gather(diag_rows, "col", axis=0, tiled=True)
+
+    factor = factor.reshape(N, -1)
+    rhs_part = jnp.concatenate(
+        [times(factor, trail_factor, ((1,), (1,))), times(factor, cand_solved, ((1,), (0,)))], axis=1
+    )
+    rhs_parts = lax.all_to_all(rhs_part.astype(bf16).reshape(cols, 64, BLK), "col", 0, 0)
+    rhs_sum = jnp.sum(rhs_parts.astype(f32), axis=0)
+    points_t = points_t[:, :BLK]
     inner = lax.dot_general(own_t, points_t, (((0,), (0,)), ((), ())), preferred_element_type=f32)
-    kernel_tile = matern(inner, norms(own_t), norms(points_t))
-
-    diag_part = times(all_factor, block_factor, ((1,), (1,)))
-    rhs_part = jnp.concatenate(
-        [
-            times(all_factor, trail_factor, ((1,), (1,))),
-            times(all_factor, cand_solved, ((1,), (0,))),
-        ],
-        axis=1,
-    )
-    column_ids = col_index * 64 + jnp.arange(64, dtype=jnp.int32)
-    row_ids = row_index * 32 + jnp.arange(32, dtype=jnp.int32)
-    on_diagonal = column_ids[:, None] == row_ids[None, :]
-    diag_tile = kernel_tile[:, 128:] - sum_scatter(diag_part, "col", cols)
-    diag_tile = diag_tile + jnp.where(on_diagonal, noise[None, :], 0.0)
-    diag_rows = spread(diag_tile, "row", rows).transpose(1, 0, 2).reshape(64, N)
-    diag_rows, rhs_part = lax.optimization_barrier((diag_rows, rhs_part))
-    whole = lax.all_gather(diag_rows, "col", axis=0, tiled=True)
-    rhs_tile = kernel_tile[:, :128] - sum_scatter(rhs_part, "col", cols)
+    rhs_tile = matern(inner, own_norms, norms(points_t)) - rhs_sum
     rhs = lax.all_gather(rhs_tile, "col", axis=0, tiled=True)
     diag_out, solved = chol_solve(col_index.reshape(1).astype(jnp.int32), whole, rhs)
     return (diag_out, solved[:, :64], solved[:, 64:])

time: 242 us -> 225 us (0.930)
  blocking collectives: 64.5 us -> 35.9 us
  waiting for transfers between devices: 28.3 us -> 53.2 us
  starting transfers between devices: 52.2 us -> 38.3 us
    all_to_all x3, waiting for transfers between devices: 10 us -> 38.7 us  [spread(): return lax.all_to_all(lax.optimization_barrier(copies), axis, 0, 0)]
    all_gather x1 -> x0, blocking collectives: 20.1 us -> none  [body(): lax.all_gather(jnp.concatenate([trail_points.T, cand_points.T, local_t],...]
    all_to_all x3, starting transfers between devices: 39.2 us -> 25.9 us  [spread(): return lax.all_to_all(lax.optimization_barrier(copies), axis, 0, 0)]
    all_to_all x1, blocking collectives: 26.5 us -> 17.9 us  [body(): lax.all_to_all(rhs_part.astype(bf16).reshape(cols, 64, BLK), 'col', 0, 0)]
    ppermute x2 -> x1, starting transfers between devices: 7.98 us -> 0.67 us  [body(): partner_t = lax.ppermute(half, ('row', 'col'), hop)]
    all_to_all x1, starting transfers between devices: 4.95 us -> 11.7 us  [body(): diag_sum = jnp.sum(lax.all_to_all(diag_part, 'col', 0, 0), axis=0)]
    ppermute x2 -> x1, waiting for transfers between devices: 6.22 us -> 0.01 us  [body(): partner_t = lax.ppermute(half, ('row', 'col'), hop)]
  transfers between devices with their start and end apart: 7 -> 7, of which waited for: 4 -> 5; matrix products, arithmetic and copies ran while one was open for 2% -> 6% of each run, Pallas kernels for 0% -> 0%
where the time goes in v2:
time: 225 us
  Pallas kernels  66 us (29%)
  waiting for transfers between devices  53.2 us (24%)
  starting transfers between devices  38.3 us (17%)
  blocking collectives  35.9 us (16%)
  between operations  14.3 us (6%)
  local copies, waits for them, and re-layouts  9.82 us (4%)
  other arithmetic  4.66 us (2%)
  matrix products  2.4 us (1%)
    pallas_call x1, Pallas kernels, chol_solve(): pl.pallas_call(kernel, out_shape=(jax.ShapeDtypeStruct((64, N), f32), jax...  66 us
    all_to_all x3, waiting for transfers between devices, spread(): return lax.all_to_all(lax.optimization_barrier(copies), axis, 0, 0)  38.7 us
    all_to_all x3, starting transfers between devices, spread(): return lax.all_to_all(lax.optimization_barrier(copies), axis, 0, 0)  25.9 us
    all_to_all x1, blocking collectives, body(): lax.all_to_all(rhs_part.astype(bf16).reshape(cols, 64, BLK), 'col', 0, 0)  17.9 us
    all_gather x1, blocking collectives, body(): rhs = lax.all_gather(rhs_tile, 'col', axis=0, tiled=True)  17.9 us
    all_to_all x1, starting transfers between devices, body(): diag_sum = jnp.sum(lax.all_to_all(diag_part, 'col', 0, 0), axis=0)  11.7 us
    all_to_all x1, waiting for transfers between devices, body(): diag_sum = jnp.sum(lax.all_to_all(diag_part, 'col', 0, 0), axis=0)  9.59 us
    all_gather x1, waiting for transfers between devices, body(): whole = lax.all_gather(diag_rows, 'col', axis=0, tiled=True)  4.79 us
  transfers between devices with their start and end apart: 7, of which 5 were waited for; matrix products, arithmetic and copies ran while one was open for 6% of the time, Pallas kernels for 0%

profile of v2, /device:TPU:1, one launch (start us, length us, event | category | flops | bytes accessed | tf_op | source)
XLA Modules:
  0.0 224.5 jit_solution(2429997684913537132)
XLA Ops:
  7.2 1.6 broadcast_in_dim.22
  8.8 13.8 %all-to-all-start = ((bf16[32,80,64]{1,2,0:T(8,128)(2,1)}), bf16[32,80,64]{1,2,0:T(8,128)(2,1)S(1)}, u32[]{:S(2)}, u32[]{:S(2)}) async-start(bf16[32,80,64]{1,2,0:T(8,128)(2,1)} %broadcast_in_dim.22), calls=%async_computation | async-start | bytes 1048576 | tf_op jit(solution)/shard_map/all_to_all | solution.py:168
  22.7 0.8 broadcast_in_dim.27
  23.5 13.4 %all-to-all-done = bf16[32,80,64]{1,2,0:T(8,128)(2,1)S(1)} async-done(((bf16[32,80,64]{1,2,0:T(8,128)(2,1)}), bf16[32,80,64]{1,2,0:T(8,128)(2,1)S(1)}, u32[]{:S(2)}, u32[]{:S(2)}) %all-to-all-start) | async-done | bytes 327712 | tf_op jit(solution)/shard_map/all_to_all | solution.py:168
  37.0 7.5 %all-to-all-start.1 = ((bf16[32,32,256]{2,1,0:T(8,128)(2,1)}), bf16[32,32,256]{2,1,0:T(8,128)(2,1)S(1)}, u32[]{:S(2)}, u32[]{:S(2)}) async-start(bf16[32,32,256]{2,1,0:T(8,128)(2,1)} %broadcast_in_dim.27), calls=%async_computation.1 | async-start | bytes 1048576 | tf_op jit(solution)/shard_map/all_to_all | solution.py:168
  44.8 0.7 maximum_maximum_fusion
  45.8 0.3 copy.31
  46.1 0.8 reshape.36
  47.0 0.7 collective-permute-start
  47.7 10.4 %all-to-all-done.1 = bf16[32,32,256]{2,1,0:T(8,128)(2,1)S(1)} async-done(((bf16[32,32,256]{2,1,0:T(8,128)(2,1)}), bf16[32,32,256]{2,1,0:T(8,128)(2,1)S(1)}, u32[]{:S(2)}, u32[]{:S(2)}) %all-to-all-start.1) | async-done | bytes 524320 | tf_op jit(solution)/shard_map/all_to_all | solution.py:168
  58.1 0.3 fusion.18
  58.4 0.8 reshape.42
  59.2 11.7 %all-to-all-start.2 = ((f32[16,1,2048]{2,1,0:T(1,128)}), f32[16,1,2048]{2,1,0:T(1,128)S(1)}, u32[]{:S(2)}, u32[]{:S(2)}) async-start(f32[16,1,2048]{2,1,0:T(1,128)} %reshape.42), calls=%async_computation.2 | async-start | bytes 262144 | tf_op jit(solution)/shard_map/all_to_all | solution.py:211
  70.9 0.2 multiply_reduce_fusion.1
  71.3 9.6 %all-to-all-done.2 = f32[16,1,2048]{2,1,0:T(1,128)S(1)} async-done(((f32[16,1,2048]{2,1,0:T(1,128)}), f32[16,1,2048]{2,1,0:T(1,128)S(1)}, u32[]{:S(2)}, u32[]{:S(2)}) %all-to-all-start.2) | async-done | bytes 131104 | tf_op jit(solution)/shard_map/all_to_all | solution.py:211
  80.8 0.5 broadcast.23
  81.4 0.9 reduce.3
  82.5 0.2 multiply_subtract_fusion.1
  82.8 0.9 broadcast_in_dim.51
  83.6 4.6 %all-to-all-start.3 = ((f32[32,72,32]{1,2,0:T(8,128)}), f32[32,72,32]{1,2,0:T(8,128)S(1)}, u32[]{:S(2)}, u32[]{:S(2)}) async-start(f32[32,72,32]{1,2,0:T(8,128)} %broadcast_in_dim.51), calls=%async_computation.3 | async-start | bytes 1048576 | tf_op jit(solution)/shard_map/all_to_all | solution.py:168
  88.3 14.9 %all-to-all-done.3 = f32[32,72,32]{1,2,0:T(8,128)S(1)} async-done(((f32[32,72,32]{1,2,0:T(8,128)}), f32[32,72,32]{1,2,0:T(8,128)S(1)}, u32[]{:S(2)}, u32[]{:S(2)}) %all-to-all-start.3) | async-done | bytes 294944 | tf_op jit(solution)/shard_map/all_to_all | solution.py:168
  103.7 0.8 select_add_fusion
  104.5 0.3 convolution_convert_fusion
  104.8 0.3 convolution_convert_fusion.1
  105.3 17.9 %all_to_all.25 = bf16[16,64,128]{2,1,0:T(8,128)(2,1)S(1)} all-to-all(bf16[16,64,128]{2,1,0:T(8,128)(2,1)S(1)} %pad_maximum_fusion), channel_id=1, replica_groups=mesh['row'=32,'col'=16] {'col'}, dimensions={0} | all-to-all | bytes 524288 | tf_op jit(solution)/shard_map/all_to_all | solution.py:228
  123.3 1.5 multiply_reduce_fusion
  124.7 1.4 multiply_subtract_fusion
  126.1 17.9 %all_gather.11.rhs_ref = f32[1024,128]{1,0:T(8,128)S(1)} all-gather(f32[64,128]{1,0:T(8,128)S(1)} %multiply_subtract_fusion), channel_id=1, replica_groups=mesh['row'=32,'col'=16] {'col'}, dimensions={0}, use_global_device_ids=true | all-gather | bytes 557056 | tf_op jit(solution)/shard_map/all_gather | solution.py:233
  144.0 4.8 %all-gather.3.cloned.1.call-done.a_ref = f32[1024,1024]{1,0:T(8,128)} async-done(((f32[64,1024]{1,0:T(8,128)}), f32[1024,1024]{1,0:T(8,128)}) %all-gather.3.cloned.1.call-update) | async-done | bytes 4194320 | tf_op jit(solution)/shard_map/all_gather | solution.py:222
  148.8 2.2 copy-done
  151.0 66.0 %shard_map.94 = (f32[64,1024]{1,0:T(8,128)}, f32[64,128]{1,0:T(8,128)S(1)}) custom-call(s32[1]{0:T(128)} %bitcast.c_ref, f32[1024,1024]{1,0:T(8,128)S(1)} %copy-done, f32[1024,128]{1,0:T(8,128)S(1)} %all_gather.11.rhs_ref), custom_call_target="tpu_custom_call" | custom-call | flops 3000000000 | bytes 5000000 | tf_op jit(solution)/shard_map/pallas_call | solution.py:150
  217.0 0.7 fusion.17
  (38 shorter events, 1.7 us)
Async XLA Ops:
  7.2 15.5 %copy-start.3 = (f32[32,256]{1,0:T(8,128)S(1)}, f32[32,256]{1,0:T(8,128)}, u32[]{:S(2)}) copy-start(f32[32,256]{1,0:T(8,128)} %param.11) | copy-start | bytes 98308
  8.8 35.7 %copy-start.4 = (bf16[64,160]{1,0:T(8,128)(2,1)S(1)}, bf16[64,160]{1,0:T(8,128)(2,1)}, u32[]{:S(2)}) copy-start(bf16[64,160]{1,0:T(8,128)(2,1)} %param.7) | copy-start | bytes 61444
  8.8 35.8 %copy-start.5 = (bf16[64,160]{1,0:T(8,128)(2,1)S(1)}, bf16[64,160]{1,0:T(8,128)(2,1)}, u32[]{:S(2)}) copy-start(bf16[64,160]{1,0:T(8,128)(2,1)} %param.9) | copy-start | bytes 61444
  8.8 28.2 %all-to-all-start = ((bf16[32,80,64]{1,2,0:T(8,128)(2,1)}), bf16[32,80,64]{1,2,0:T(8,128)(2,1)S(1)}, u32[]{:S(2)}, u32[]{:S(2)}) async-start(bf16[32,80,64]{1,2,0:T(8,128)(2,1)} %broadcast_in_dim.22), calls=%async_computation | async-start | bytes 1048576 | tf_op jit(solution)/shard_map/all_to_all | solution.py:168
  22.7 22.9 %copy-start.6 = (f32[32]{0:T(128)S(1)}, f32[32]{0:T(128)}, u32[]{:S(2)}) copy-start(f32[32]{0:T(128)} %param.13) | copy-start | bytes 388
  37.0 21.1 %all-to-all-start.1 = ((bf16[32,32,256]{2,1,0:T(8,128)(2,1)}), bf16[32,32,256]{2,1,0:T(8,128)(2,1)S(1)}, u32[]{:S(2)}, u32[]{:S(2)}) async-start(bf16[32,32,256]{2,1,0:T(8,128)(2,1)} %broadcast_in_dim.27), calls=%async_computation.1 | async-start | bytes 1048576 | tf_op jit(solution)/shard_map/all_to_all | solution.py:168
  44.5 78.8 %all-gather.5.cloned.1.call-start = ((), (), s32[]{:S(2)}) async-start(), calls=%async_computation.6 | async-start | bytes 1392640 | tf_op jit(solution)/shard_map/all_gather | solution.py:192
  47.0 24.1 %collective-permute-start = (bf16[2560,32]{0,1:T(8,128)(2,1)S(1)}, bf16[2560,32]{0,1:T(8,128)(2,1)S(1)}, u32[]{:S(2)}, u32[]{:S(2)}) collective-permute-start(bf16[2560,32]{0,1:T(8,128)(2,1)S(1)} %slice_select_fusion), channel_id=1, source_target_pairs={{0,0},{1,1},{2,2},{3,3},{4,4},{5,5},{6,6},{7,7},{8,8},{9,9},{10,10... | collective-permute-start | bytes 491528 | tf_op jit(solution)/shard_map/ppermute | solution.py:201
  59.2 21.7 %all-to-all-start.2 = ((f32[16,1,2048]{2,1,0:T(1,128)}), f32[16,1,2048]{2,1,0:T(1,128)S(1)}, u32[]{:S(2)}, u32[]{:S(2)}) async-start(f32[16,1,2048]{2,1,0:T(1,128)} %reshape.42), calls=%async_computation.2 | async-start | bytes 262144 | tf_op jit(solution)/shard_map/all_to_all | solution.py:211
  83.6 19.5 %all-to-all-start.3 = ((f32[32,72,32]{1,2,0:T(8,128)}), f32[32,72,32]{1,2,0:T(8,128)S(1)}, u32[]{:S(2)}, u32[]{:S(2)}) async-start(f32[32,72,32]{1,2,0:T(8,128)} %broadcast_in_dim.51), calls=%async_computation.3 | async-start | bytes 1048576 | tf_op jit(solution)/shard_map/all_to_all | solution.py:168
  88.2 60.6 %all-gather.3.cloned.1.call-start = ((), (), s32[]{:S(2)}) async-start(), calls=%async_computation.5 | async-start | bytes 4456448 | tf_op jit(solution)/shard_map/all_gather | solution.py:222
  88.3 16.3 %copy-start.1 = (f32[256,64]{0,1:T(8,128)S(1)}, f32[256,64]{0,1:T(8,128)}, u32[]{:S(2)}) copy-start(f32[256,64]{0,1:T(8,128)} %param.12) | copy-start | bytes 196612
  103.3 1.5 copy-start.2
  148.8 2.2 copy-start
Sparse Core Ops, SparseCore 0:
  47.4 44.3 all-gather.4
  104.6 44.1 all-gather.2

commit v3 on v2

v3 whole, which is shorter than its diff:
```python
import functools

import jax
import jax.numpy as jnp
from jax import lax
from jax.experimental import pallas as pl
from jax.experimental.pallas import tpu as pltpu
from jax.sharding import PartitionSpec as P

D = 2560
PAD = 128

N = 1024
BLK = 128
f32, bf16 = jnp.float32, jnp.bfloat16


def split(x):
    high = x.astype(bf16)
    return high, (x - high.astype(f32)).astype(bf16)


def mm(a, b, bt=False):
    dims = (((1,), (1 if bt else 0,)), ((), ()))
    return lax.dot_general(a, b, dims, preferred_element_type=f32)


def left(x):
    high, low = split(x)
    return jnp.concatenate([high, high, low], axis=1)


def right(x, axis=1):
    high, low = split(x)
    return jnp.concatenate([high, low, high], axis=axis)


def rows_of(x):
    return [jnp.broadcast_to(x[k : k + 1, :], (8, BLK)) for k in range(8)]


def lane(x, j):
    return jnp.broadcast_to(x[:, j : j + 1], (8, BLK))


def recip(x):
    r = pl.reciprocal(x, approx=True)
    return r * (2.0 - x * r)


def tree(terms):
    while len(terms) > 1:
        terms = [sum(terms[i : i + 2][1:], terms[i]) for i in range(0, len(terms), 2)]
    return terms[0]


def factor_inverse(D, store):
    sub = lax.broadcasted_iota(jnp.int32, (8, BLK), 0)
    ln = lax.broadcasted_iota(jnp.int32, (8, BLK), 1)
    E = [jnp.where(sub + 8 * v == ln, 1.0, 0.0).astype(f32) for v in range(16)]
    for g in range(16):
        R, RE = rows_of(D[g]), rows_of(E[g])
        G = {}
        for i in range(8):
            for l in range(i, 8):
                G[i, l] = lane(R[i], 8 * g + l)
        M = {v: [lane(D[v], 8 * g + k) for k in range(8)] for v in range(g + 1, 16)}
        X = list(M[g + 1]) if g < 15 else None
        C, Z, ZE, out = {}, [None] * 8, [None] * 8, None
        for i in range(0, 8, 2):
            p, q, s = G[i, i], G[i, i + 1], G[i + 1, i + 1]
            det = p * s - q * q
            inv = 1.0 / det
            first, last = {}, {}
            for l in range(i + 2, 8):
                first[l] = s * G[i, l] - q * G[i + 1, l]
                last[l] = p * G[i + 1, l] - q * G[i, l]
            for l in range(i + 2, 8):
                for m in range(l, 8):
                    G[l, m] = G[l, m] - (G[i, m] * first[l] + G[i + 1, m] * last[l]) * inv
            pinv, sinv, qinv = p * inv, s * inv, q * inv
            Z[i], Z[i + 1] = sinv * R[i] - qinv * R[i + 1], pinv * R[i + 1] - qinv * R[i]
            ZE[i], ZE[i + 1] = sinv * RE[i] - qinv * RE[i + 1], pinv * RE[i + 1] - qinv * RE[i]
            for l in range(i + 2, 8):
                C[l, i], C[l, i + 1] = first[l] * inv, last[l] * inv
                R[l] = R[l] - (C[l, i] * R[i] + C[l, i + 1] * R[i + 1])
                RE[l] = RE[l] - (C[l, i] * RE[i] + C[l, i + 1] * RE[i + 1])
                if X:
                    X[l] = X[l] - (C[l, i] * X[i] + C[l, i + 1] * X[i + 1])
            ratio = 1.0 / p
            even = RE[i] * lax.rsqrt(p)
            odd = (RE[i + 1] - (q * ratio) * RE[i]) * lax.rsqrt(det * ratio)
            out = even if out is None else jnp.where(sub == i, even, out)
            out = jnp.where(sub == i + 1, odd, out)
        store(g, out)
        if g == 15:
            break
        d = D[g + 1] - tree([X[k] * Z[k] for k in range(6)])
        D[g + 1] = d - (X[6] * Z[6] + X[7] * Z[7])
        E[g + 1] = E[g + 1] - tree([X[k] * ZE[k] for k in range(8)])
        V, VE = [None] * 8, [None] * 8
        for i in range(7, -1, -1):
            low = i + 2 - i % 2
            V[i], VE[i] = Z[i], ZE[i]
            if low < 8:
                V[i] = V[i] - tree([C[l, i] * V[l] for l in range(low, 8)])
                VE[i] = VE[i] - tree([C[l, i] * VE[l] for l in range(low, 8)])
        for v in range(g + 2, 16):
            D[v] = D[v] - tree([M[v][k] * V[k] for k in range(8)])
            E[v] = E[v] - tree([M[v][k] * VE[k] for k in range(8)])


def eliminate(i, t, rt, pa, pb, inverse, solved):
    start = (i + 1) * BLK
    if start == N:
        return
    panel = mm(left(t[start:, i * BLK : start]), inverse, True)
    pa[start:, :] = left(panel)
    pb[start:, :] = right(panel)
    rt[start:, :] -= mm(pa[start:, :], solved)
    first = start
    while first < N:
        wide = 256 if (N - first) % 256 == 0 else 128
        t[first:, first : first + wide] -= mm(pa[first:, :], pb[first : first + wide, :], True)
        first += wide


def kernel(c_ref, a_ref, rhs_ref, diag_ref, panel_ref, cand_ref, t, rt, linv, pa, pb, sems):
    copies = []
    for k in range(8):
        rows = pl.ds(k * BLK, BLK)
        edge = N - k * BLK
        pieces = [(0, k * BLK, edge)] + ([(edge, 0, k * BLK)] if k else [])
        for source, target, width in pieces:
            copies.append(
                pltpu.make_async_copy(
                    a_ref.at[rows, pl.ds(source, width)],
                    t.at[rows, pl.ds(target, width)],
                    sems.at[len(copies)],
                )
            )
            copies[-1].start()
    mine = pl.multiple_of(c_ref[0] * 64, 64)
    rt[...] = rhs_ref[...]
    copies[0].wait()

    def step(kb, _):
        base = pl.multiple_of(kb * BLK, BLK)
        D = [t[pl.ds(pl.multiple_of(base + 8 * v, 8), 8), pl.ds(base, BLK)] for v in range(16)]

        def store(g, rows):
            linv[8 * g : 8 * g + 8, :] = rows

        factor_inverse(D, store)

        @pl.when(kb == 0)
        def _():
            for copy in copies[1:]:
                copy.wait()

        inverse = right(linv[...])
        low = mm(left(t[pl.ds(mine, 64), pl.ds(base, BLK)]), inverse, True)
        ri = lax.broadcasted_iota(jnp.int32, (64, BLK), 0) + mine
        ci = lax.broadcasted_iota(jnp.int32, (64, BLK), 1) + base
        diag_ref[:, pl.ds(base, BLK)] = jnp.where(ri >= ci, low, 0.0)
        solved = mm(left(linv[...]), right(rt[pl.ds(base, BLK), :], 0))
        rt[pl.ds(base, BLK), :] = solved
        solved = right(solved, 0)
        for i in range(8):
            pl.when(kb == i)(functools.partial(eliminate, i, t, rt, pa, pb, inverse, solved))
        return 0

    lax.fori_loop(0, 8, step, 0)
    panel_ref[...] = rt[pl.ds(mine, 64), :64]
    cand_ref[...] = rt[pl.ds(mine, 64), 64:]


def chol_solve(c, a, rhs):
    return pl.pallas_call(
        kernel,
        out_shape=(
            jax.ShapeDtypeStruct((64, N), f32),
            jax.ShapeDtypeStruct((64, 64), f32),
            jax.ShapeDtypeStruct((64, 64), f32),
        ),
        in_specs=[
            pl.BlockSpec(memory_space=pltpu.SMEM),
            pl.BlockSpec(memory_space=pl.ANY),
            pl.BlockSpec(memory_space=pltpu.VMEM),
        ],
        out_specs=(pl.BlockSpec(memory_space=pltpu.VMEM),) * 3,
        scratch_shapes=[
            pltpu.VMEM((N, N), f32),
            pltpu.VMEM((N, BLK), f32),
            pltpu.VMEM((BLK, BLK), f32),
            pltpu.VMEM((N, 3 * BLK), bf16),
            pltpu.VMEM((N, 3 * BLK), bf16),
            pltpu.SemaphoreType.DMA((15,)),
        ],
        compiler_params=pltpu.CompilerParams(vmem_limit_bytes=60 * 1024 * 1024),
        cost_estimate=pl.CostEstimate(flops=3 * 10**9, bytes_accessed=5 * 10**6, transcendentals=0),
    )(c, a, rhs)


SMALL = pltpu.CompilerParams(vmem_limit_bytes=8 * 1024 * 1024)


def slab_kernel(c_ref, tiles_ref, out_ref):
    swap = c_ref[0] % 2
    place = lax.broadcasted_iota(jnp.int32, (16, BLK), 1) // 32
    for d in range(8):
        four = []
        for side in range(2):
            for half in range(2):
                four.append(tiles_ref[4 * d + 2 * (side + swap - 2 * side * swap) + half])
        for q in range(4):
            piece = four[0] if q == 0 else pltpu.roll(four[0], BLK - 32 * q, 1)
            for k in range(1, 4):
                turn = (32 * (k - q)) % BLK
                piece = jnp.where(place == k, pltpu.roll(four[k], turn, 1) if turn else four[k], piece)
            out_ref[16 * q : 16 * q + 16, BLK * d : BLK * d + BLK] = piece


def row_slab(c, tiles):
    return pl.pallas_call(
        slab_kernel,
        out_shape=jax.ShapeDtypeStruct((64, N), f32),
        in_specs=[pl.BlockSpec(memory_space=pltpu.SMEM), pl.BlockSpec(memory_space=pltpu.VMEM)],
        out_specs=pl.BlockSpec(memory_space=pltpu.VMEM),
        compiler_params=SMALL,
    )(c, tiles)


def product_kernel(place_ref, packed_ref, out_ref):
    distance, side, half = place_ref[0], place_ref[1], place_ref[2]
    lanes = lax.broadcasted_iota(jnp.int32, (16, BLK), 1) // 32
    for c in range(16):
        other = 2 * ((c // 2 + distance) % 8) + (side + c) % 2
        total = None
        for part in range(2):
            at = slice(32 * part, 32 * part + 32)
            left_rows = jnp.concatenate([packed_ref[2 * c, at, :], packed_ref[2 * c + 1, at, :]], axis=0)
            right_rows = packed_ref[2 * other + half, at, :]
            one = mm(left_rows, jnp.concatenate([right_rows] * 4, axis=0), True)
            total = one if total is None else total + one
        piece = total[:16]
        for q in range(1, 4):
            piece = jnp.where(lanes == q, total[16 * q : 16 * q + 16], piece)
        out_ref[c] = piece


def tile_products(place, packed):
    return pl.pallas_call(
        product_kernel,
        out_shape=jax.ShapeDtypeStruct((16, 16, BLK), f32),
        in_specs=[pl.BlockSpec(memory_space=pltpu.SMEM), pl.BlockSpec(memory_space=pltpu.VMEM)],
        out_specs=pl.BlockSpec(memory_space=pltpu.VMEM),
        compiler_params=SMALL,
    )(place, packed)


def finish_kernel(parts_ref, tile_ref, out_ref):
    total = tree([parts_ref[c] for c in range(16)])
    result = tile_ref[...] - total
    for r in range(32):
        out_ref[r] = result


def finish_tile(parts, tile):
    return pl.pallas_call(
        finish_kernel,
        out_shape=jax.ShapeDtypeStruct((32, 16, BLK), f32),
        in_specs=[pl.BlockSpec(memory_space=pltpu.VMEM), pl.BlockSpec(memory_space=pltpu.VMEM)],
        out_specs=pl.BlockSpec(memory_space=pltpu.VMEM),
        compiler_params=SMALL,
    )(parts, tile)


def spread(value, axis, count):
    copies = jnp.broadcast_to(value[None], (count,) + value.shape)
    return lax.all_to_all(lax.optimization_barrier(copies), axis, 0, 0)


def matern(inner, left_norms, right_norms):
    squared = jnp.maximum(left_norms[:, None] + right_norms[None, :] - 2.0 * inner, 0.0)
    scaled = jnp.sqrt(5.0 * squared / D)
    return (1.0 + scaled + scaled * scaled / 3.0) * jnp.exp(-scaled)


def norms(points):
    return jnp.sum(jnp.square(points.astype(f32)), axis=0)


def times(a, b, dims):
    return lax.dot_general(a, b.astype(bf16), (dims, ((), ())), preferred_element_type=f32)


def body(trail_points, block_points, cand_points, trail_factor, block_factor, cand_solved, noise):
    rows, cols = 32, 16
    row_index = lax.axis_index("row")
    col_index = lax.axis_index("col")
    odd = row_index % 2
    side = row_index // 2 % 2
    distance = row_index // 4
    pad = jnp.zeros((trail_points.shape[1], PAD), bf16)
    points_t = lax.all_gather(
        jnp.concatenate([trail_points.T, cand_points.T, pad], axis=1), "col", axis=0, tiled=True
    )
    block_t = block_points.T
    flat = block_factor.astype(bf16)
    packed = jnp.concatenate(
        [flat[:, :BLK], flat[:, BLK:], jnp.concatenate([block_t[:40], block_t[40:]], axis=1)], axis=0
    )
    packed = spread(packed, "row", rows)
    settle = [((2 * c + h) * cols + c, h * cols + c) for c in range(cols) for h in range(2)]
    own_noise = lax.ppermute(noise, ("row", "col"), settle)
    hop = []
    for r in range(rows):
        for c in range(cols):
            partner = 2 * ((c // 2 + r // 4) % 8) + (r // 2 + c) % 2
            hop.append((r * cols + partner, r * cols + c))
    own = packed[:, 64:, :].reshape(D // 2, BLK)
    partner = lax.ppermute(own, ("row", "col"), hop)
    place = jnp.stack([distance, side, odd]).astype(jnp.int32)
    parts = lax.all_to_all(tile_products(place, packed), "col", 0, 0)
    own_norms = norms(own)
    own_norms = own_norms[:64] + own_norms[64:]
    partner_norms = norms(partner)
    partner_norms = partner_norms[:64] + partner_norms[64:]
    inner = lax.dot_general(own, partner, (((0,), (0,)), ((), ())), preferred_element_type=f32)
    tile = matern(inner[:64, :64] + inner[64:, 64:], own_norms, partner_norms)
    tile = jnp.where(odd == 0, tile[:, :32], tile[:, 32:])
    line = jnp.arange(64, dtype=jnp.int32)[:, None] - 32 * odd
    tile = tile + jnp.where(line == jnp.arange(32, dtype=jnp.int32)[None, :], own_noise[None, :], 0.0)
    tile = jnp.concatenate([tile[16 * q : 16 * q + 16] for q in range(4)], axis=1)
    sent = finish_tile(parts, lax.optimization_barrier(tile))
    diag_rows = row_slab(col_index.reshape(1), lax.all_to_all(sent, "row", 0, 0))
    diag_rows, packed = lax.optimization_barrier((diag_rows, packed))
    whole = lax.all_gather(diag_rows, "col", axis=0, tiled=True)

    factor = jnp.concatenate([packed[:, :32], packed[:, 32:64]], axis=2).reshape(N, -1)
    rhs_part = jnp.concatenate(
        [times(factor, trail_factor, ((1,), (1,))), times(factor, cand_solved, ((1,), (0,)))], axis=1
    )
    rhs_parts = lax.all_to_all(rhs_part.astype(bf16).reshape(cols, 64, BLK), "col", 0, 0)
    rhs_sum = jnp.sum(rhs_parts.astype(f32), axis=0)
    points_t = points_t[:, :BLK]
    own_t = jnp.stack([packed[:, 64:, :64], packed[:, 64:, 64:]], axis=1).reshape(D, -1)
    inner = lax.dot_general(own_t, points_t, (((0,), (0,)), ((), ())), preferred_element_type=f32)
    rhs_tile = matern(inner, own_norms, norms(points_t)) - rhs_sum
    rhs = lax.all_gather(rhs_tile, "col", axis=0, tiled=True)
    return chol_solve(col_index.reshape(1).astype(jnp.int32), whole, rhs)


def solution(mesh):
    return jax.shard_map(
        body,
        mesh=mesh,
        in_specs=(
            P("row", "col"),
            P("col", "row"),
            P("row", "col"),
            P("row", "col"),
            P("row", "col"),
            P("col", "row"),
            P("row"),
        ),
        out_specs=(P("col", None), P("col", "row"), P("col", "row")),
        check_vma=False,
    )
```

time: 225 us -> 196 us (0.87)
  Pallas kernels: 66 us -> 43.9 us
  starting transfers between devices: 38.3 us -> 57.3 us
  blocking collectives: 35.9 us -> 19.4 us
  local copies, waits for them, and re-layouts: 9.82 us -> 3.05 us
    all_to_all x1 -> x3, starting transfers between devices: 11.7 us -> 41.5 us  [the longest x1 20.7 us: body(): lax.all_to_all(sent, 'row', 0, 0)]
    pallas_call x1, Pallas kernels: 66 us -> 40.2 us  [chol_solve(): pl.pallas_call(kernel, out_shape=(jax.ShapeDtypeStruct((64, N), f32), jax...]
    all_to_all x3 -> x1, waiting for transfers between devices: 38.7 us -> 17.8 us  [spread(): return lax.all_to_all(lax.optimization_barrier(copies), axis, 0, 0)]
    all_to_all x1 -> x3, waiting for transfers between devices: 9.59 us -> 29.8 us  [the longest x1 12.2 us: body(): lax.all_to_all(rhs_part.astype(bf16).reshape(cols, 64, BLK), 'col', 0, 0)]
    all_to_all x1 -> x0, blocking collectives: 17.9 us -> none  [body(): lax.all_to_all(rhs_part.astype(bf16).reshape(cols, 64, BLK), 'col', 0, 0)]
    all_to_all x3 -> x1, starting transfers between devices: 25.9 us -> 13.7 us  [spread(): return lax.all_to_all(lax.optimization_barrier(copies), axis, 0, 0)]
    pallas_call x0 -> x3, Pallas kernels: none -> 3.66 us  [the longest x1 1.96 us: tile_products(): pl.pallas_call(product_kernel, out_shape=jax.ShapeDtypeStruct((16, 16, BL...]
    broadcast_in_dim x3 -> x1, local copies, waits for them, and re-layouts: 3.33 us -> 1.02 us  [spread(): copies = jnp.broadcast_to(value[None], (count,) + value.shape)]
  transfers between devices with their start and end apart: 7 -> 8, of which waited for: 5 -> 5; matrix products, arithmetic and copies ran while one was open for 6% -> 3% of each run, Pallas kernels for 0% -> 2%
where the time goes in v3:
time: 196 us; the launch traced here: 195 us
  starting transfers between devices  57.3 us (29%)
  waiting for transfers between devices  51.3 us (26%)
  Pallas kernels  43.9 us (22%)
  blocking collectives  19.4 us (10%)
  between operations  14.4 us (7%)
  other arithmetic  5.01 us (3%)
  local copies, waits for them, and re-layouts  3.05 us (2%)
    pallas_call x1, Pallas kernels, chol_solve(): pl.pallas_call(kernel, out_shape=(jax.ShapeDtypeStruct((64, N), f32), jax...  40.2 us
    all_to_all x1, starting transfers between devices, body(): lax.all_to_all(sent, 'row', 0, 0)  20.7 us
    all_gather x1, blocking collectives, body(): rhs = lax.all_gather(rhs_tile, 'col', axis=0, tiled=True)  19.4 us
    all_to_all x1, waiting for transfers between devices, spread(): return lax.all_to_all(lax.optimization_barrier(copies), axis, 0, 0)  17.8 us
    all_to_all x1, starting transfers between devices, spread(): return lax.all_to_all(lax.optimization_barrier(copies), axis, 0, 0)  13.7 us
    all_to_all x1, starting transfers between devices, body(): parts = lax.all_to_all(tile_products(place, packed), 'col', 0, 0)  12.5 us
    all_to_all x1, waiting for transfers between devices, body(): lax.all_to_all(rhs_part.astype(bf16).reshape(cols, 64, BLK), 'col', 0, 0)  12.2 us
    all_to_all x1, waiting for transfers between devices, body(): lax.all_to_all(sent, 'row', 0, 0)  9.63 us
  transfers between devices with their start and end apart: 8, of which 5 were waited for; matrix products, arithmetic and copies ran while one was open for 3% of the time, Pallas kernels for 2%

profile of v3, /device:TPU:1, one launch (start us, length us, event | category | flops | bytes accessed | tf_op | source)
XLA Modules:
  0.0 195.5 jit_solution(15166451937814197593)
XLA Ops:
  7.2 0.8 copy.31
  8.0 0.8 convert_element_type.24
  8.9 1.0 broadcast_in_dim.12
  9.9 13.7 %all-to-all-start = ((bf16[32,104,128]{2,1,0:T(8,128)(2,1)}), bf16[32,104,128]{2,1,0:T(8,128)(2,1)S(1)}, u32[]{:S(2)}, u32[]{:S(2)}) async-start(bf16[32,104,128]{2,1,0:T(8,128)(2,1)} %broadcast_in_dim.12), calls=%async_computation | async-start | bytes 1703936 | tf_op jit(solution)/shard_map/all_to_all | solution.py:281
  23.7 1.3 collective-permute-start.1
  25.1 0.1 copy.35
  25.2 0.7 maximum_maximum_fusion
  26.1 17.8 %all-to-all-done.packed_ref = bf16[32,104,128]{2,1,0:T(8,128)(2,1)S(1)} async-done(((bf16[32,104,128]{2,1,0:T(8,128)(2,1)}), bf16[32,104,128]{2,1,0:T(8,128)(2,1)S(1)}, u32[]{:S(2)}, u32[]{:S(2)}) %all-to-all-start) | async-done | bytes 852000 | tf_op jit(solution)/shard_map/all_to_all | solution.py:281
  44.0 0.7 collective-permute-start
  44.7 2.0 %shard_map.94 = f32[16,16,128]{2,1,0:T(8,128)} custom-call(s32[3]{0:T(128)S(1)} %pad_add_fusion.place_ref, bf16[32,104,128]{2,1,0:T(8,128)(2,1)S(1)} %all-to-all-done.packed_ref), custom_call_target="tpu_custom_call" | custom-call | tf_op jit(solution)/shard_map/pallas_call | solution.py:253
  46.6 12.5 %all-to-all-start.1 = ((f32[16,16,128]{2,1,0:T(8,128)}), f32[16,16,128]{2,1,0:T(8,128)S(1)}, u32[]{:S(2)}, u32[]{:S(2)}) async-start(f32[16,16,128]{2,1,0:T(8,128)} %shard_map.94), calls=%async_computation.1 | async-start | bytes 262144 | tf_op jit(solution)/shard_map/all_to_all | solution.py:325
  59.1 0.2 multiply_reduce_fusion.2
  59.4 0.2 multiply_reduce_fusion.1
  59.7 0.3 fusion.21
  60.3 8.0 %all-to-all-done.1.parts_ref = f32[16,16,128]{2,1,0:T(8,128)S(1)} async-done(((f32[16,16,128]{2,1,0:T(8,128)}), f32[16,16,128]{2,1,0:T(8,128)S(1)}, u32[]{:S(2)}, u32[]{:S(2)}) %all-to-all-start.1) | async-done | bytes 131104 | tf_op jit(solution)/shard_map/all_to_all | solution.py:325
  68.3 0.7 shard_map.95
  69.0 20.7 %all-to-all-start.2 = ((f32[32,16,128]{2,1,0:T(8,128)}), f32[32,16,128]{2,1,0:T(8,128)S(1)}, u32[]{:S(2)}, u32[]{:S(2)}) async-start(f32[32,16,128]{2,1,0:T(8,128)} %shard_map.95), calls=%async_computation.2 | async-start | bytes 524288 | tf_op jit(solution)/shard_map/all_to_all | solution.py:337
  89.8 9.6 %all-to-all-done.2.tiles_ref = f32[32,16,128]{2,1,0:T(8,128)S(1)} async-done(((f32[32,16,128]{2,1,0:T(8,128)}), f32[32,16,128]{2,1,0:T(8,128)S(1)}, u32[]{:S(2)}, u32[]{:S(2)}) %all-to-all-start.2) | async-done | bytes 262176 | tf_op jit(solution)/shard_map/all_to_all | solution.py:337
  99.4 1.0 shard_map.96
  100.5 0.7 copy-done.1
  101.2 0.3 convolution_convert_fusion
  101.5 0.3 convolution_convert_fusion.1
  101.8 0.9 pad_maximum_fusion.2
  102.7 8.3 %all-to-all-start.3 = ((bf16[16,64,128]{2,1,0:T(8,128)(2,1)}), bf16[16,64,128]{2,1,0:T(8,128)(2,1)S(1)}, u32[]{:S(2)}, u32[]{:S(2)}) async-start(bf16[16,64,128]{2,1,0:T(8,128)(2,1)} %pad_maximum_fusion.2), calls=%async_computation.3 | async-start | bytes 524288 | tf_op jit(solution)/shard_map/all_to_all | solution.py:345
  111.0 1.4 multiply_reduce_fusion
  112.4 0.2 slice_bitcast_fusion.1
  112.6 0.1 pad_maximum_fusion
  112.8 12.2 %all-to-all-done.3 = bf16[16,64,128]{2,1,0:T(8,128)(2,1)S(1)} async-done(((bf16[16,64,128]{2,1,0:T(8,128)(2,1)}), bf16[16,64,128]{2,1,0:T(8,128)(2,1)S(1)}, u32[]{:S(2)}, u32[]{:S(2)}) %all-to-all-start.3) | async-done | bytes 262176 | tf_op jit(solution)/shard_map/all_to_all | solution.py:345
  125.0 0.4 multiply_subtract_fusion
  125.4 19.4 %all_gather.11.rhs_ref = f32[1024,128]{1,0:T(8,128)} all-gather(f32[64,128]{1,0:T(8,128)S(1)} %multiply_subtract_fusion), channel_id=1, replica_groups=mesh['row'=32,'col'=16] {'col'}, dimensions={0}, use_global_device_ids=true | all-gather | bytes 557056 | tf_op jit(solution)/shard_map/all_gather | solution.py:351
  144.8 3.6 %all-gather.3.cloned.1.call-done.a_ref = f32[1024,1024]{1,0:T(8,128)} async-done(((f32[64,1024]{1,0:T(8,128)}), f32[1024,1024]{1,0:T(8,128)}) %all-gather.3.cloned.1.call-update) | async-done | bytes 4194320 | tf_op jit(solution)/shard_map/all_gather | solution.py:339
  148.4 40.2 %shard_map.97 = (f32[64,1024]{1,0:T(8,128)}, f32[64,64]{1,0:T(8,128)}, f32[64,64]{1,0:T(8,128)}) custom-call(s32[1]{0:T(128)} %bitcast.c_ref, f32[1024,1024]{1,0:T(8,128)} %all-gather.3.cloned.1.call-done.a_ref, f32[1024,128]{1,0:T(8,128)} %all_gather.11.rhs_ref), custom_call_target="tpu_custom_call" | custom-call | flops 3000000000 | bytes 5000000 | tf_op jit(solution)/shard_map/pallas_call | solution.py:179
  (37 shorter events, 1.1 us)
Async XLA Ops:
  8.8 14.9 %copy-start.5 = (f32[32]{0:T(128)S(1)}, f32[32]{0:T(128)}, u32[]{:S(2)}) copy-start(f32[32]{0:T(128)} %param.13) | copy-start | bytes 388
  8.8 16.2 %copy-start.3 = (bf16[64,160]{1,0:T(8,128)(2,1)S(1)}, bf16[64,160]{1,0:T(8,128)(2,1)}, u32[]{:S(2)}) copy-start(bf16[64,160]{1,0:T(8,128)(2,1)} %param.7) | copy-start | bytes 61444
  8.9 16.2 %copy-start.4 = (bf16[64,160]{1,0:T(8,128)(2,1)S(1)}, bf16[64,160]{1,0:T(8,128)(2,1)}, u32[]{:S(2)}) copy-start(bf16[64,160]{1,0:T(8,128)(2,1)} %param.9) | copy-start | bytes 61444
  9.9 34.1 %all-to-all-start = ((bf16[32,104,128]{2,1,0:T(8,128)(2,1)}), bf16[32,104,128]{2,1,0:T(8,128)(2,1)S(1)}, u32[]{:S(2)}, u32[]{:S(2)}) async-start(bf16[32,104,128]{2,1,0:T(8,128)(2,1)} %broadcast_in_dim.12), calls=%async_computation | async-start | bytes 1703936 | tf_op jit(solution)/shard_map/all_to_all | solution.py:281
  23.6 87.4 %all-gather.5.cloned.1.call-start = ((), (), s32[]{:S(2)}) async-start(), calls=%async_computation.5 | async-start | bytes 1392640 | tf_op jit(solution)/shard_map/all_gather | solution.py:306
  23.7 36.4 %collective-permute-start.1 = (f32[32]{0:T(128)S(1)}, f32[32]{0:T(128)S(1)}, u32[]{:S(2)}, u32[]{:S(2)}) collective-permute-start(f32[32]{0:T(128)S(1)} %copy-done.5), channel_id=1, source_target_pairs={{0,0},{16,16},{33,1},{49,17},{66,2},{82,18},{99,3},{115,19},{132,4... | collective-permute-start | bytes 392 | tf_op jit(solution)/shard_map/ppermute | solution.py:316
  44.0 15.4 %collective-permute-start = (bf16[1280,128]{1,0:T(8,128)(2,1)S(1)}, bf16[1280,128]{1,0:T(8,128)(2,1)S(1)}, u32[]{:S(2)}, u32[]{:S(2)}) collective-permute-start(bf16[1280,128]{1,0:T(8,128)(2,1)S(1)} %bitcast.28), channel_id=1, source_target_pairs={{0,0},{1,1},{2,2},{3,3},{4,4},{5,5},{6,6},{7,7},{8,8},{9,9},{10,10... | collective-permute-start | bytes 983048 | tf_op jit(solution)/shard_map/ppermute | solution.py:323
  46.6 21.6 %all-to-all-start.1 = ((f32[16,16,128]{2,1,0:T(8,128)}), f32[16,16,128]{2,1,0:T(8,128)S(1)}, u32[]{:S(2)}, u32[]{:S(2)}) async-start(f32[16,16,128]{2,1,0:T(8,128)} %shard_map.94), calls=%async_computation.1 | async-start | bytes 262144 | tf_op jit(solution)/shard_map/all_to_all | solution.py:325
  69.0 30.4 %all-to-all-start.2 = ((f32[32,16,128]{2,1,0:T(8,128)}), f32[32,16,128]{2,1,0:T(8,128)S(1)}, u32[]{:S(2)}, u32[]{:S(2)}) async-start(f32[32,16,128]{2,1,0:T(8,128)} %shard_map.95), calls=%async_computation.2 | async-start | bytes 524288 | tf_op jit(solution)/shard_map/all_to_all | solution.py:337
  89.7 58.7 %all-gather.3.cloned.1.call-start = ((), (), s32[]{:S(2)}) async-start(), calls=%async_computation.4 | async-start | bytes 4456448 | tf_op jit(solution)/shard_map/all_gather | solution.py:339
  100.4 0.8 copy-start.1
  100.4 1.1 copy-start.2
  102.7 22.3 %all-to-all-start.3 = ((bf16[16,64,128]{2,1,0:T(8,128)(2,1)}), bf16[16,64,128]{2,1,0:T(8,128)(2,1)S(1)}, u32[]{:S(2)}, u32[]{:S(2)}) async-start(bf16[16,64,128]{2,1,0:T(8,128)(2,1)} %pad_maximum_fusion.2), calls=%async_computation.3 | async-start | bytes 524288 | tf_op jit(solution)/shard_map/all_to_all | solution.py:345
  112.6 12.4 %copy-start = (bf16[2560,256]{1,0:T(8,128)(2,1)S(1)}, bf16[2560,256]{1,0:T(8,128)(2,1)}, u32[]{:S(2)}) copy-start(bf16[2560,256]{1,0:T(8,128)(2,1)} %all-gather.5.cloned.1.call-done) | copy-start | bytes 3932164
Sparse Core Ops, SparseCore 0:
  26.6 43.1 all-gather.4
  100.5 47.8 all-gather.2

commit v4 on v3

--- a/solution.py
+++ b/solution.py
@@ -231,9 +231,20 @@
     )(c, tiles)
 
 
-def product_kernel(place_ref, packed_ref, out_ref):
+def product_kernel(place_ref, packed_ref, out_ref, half_ref):
     distance, side, half = place_ref[0], place_ref[1], place_ref[2]
     lanes = lax.broadcasted_iota(jnp.int32, (16, BLK), 1) // 32
+    group = lax.broadcasted_iota(jnp.int32, (80, BLK), 1) // 32
+    for r in range(0, 16, 2):
+        upper, lower = (
+            jnp.concatenate([packed_ref[k, 64:, :].astype(f32), packed_ref[k + 1, 64:, :].astype(f32)], axis=0)
+            for k in (r, 16 + r)
+        )
+        whole = jnp.where(half == 0, upper, pltpu.roll(upper, 96, 1))
+        other = jnp.where(half == 0, pltpu.roll(lower, 64, 1), pltpu.roll(lower, 32, 1))
+        near = jnp.where(group == 0, whole, pltpu.roll(whole, 96, 1))
+        far = jnp.where(group == 2, other, pltpu.roll(other, 96, 1))
+        half_ref[40 * r : 40 * r + 80, :] = jnp.where(group < 2, near, far).astype(bf16)
     for c in range(16):
         other = 2 * ((c // 2 + distance) % 8) + (side + c) % 2
         total = None
@@ -252,9 +263,12 @@
 def tile_products(place, packed):
     return pl.pallas_call(
         product_kernel,
-        out_shape=jax.ShapeDtypeStruct((16, 16, BLK), f32),
+        out_shape=(
+            jax.ShapeDtypeStruct((16, 16, BLK), f32),
+            jax.ShapeDtypeStruct((D // 4, BLK), bf16),
+        ),
         in_specs=[pl.BlockSpec(memory_space=pltpu.SMEM), pl.BlockSpec(memory_space=pltpu.VMEM)],
-        out_specs=pl.BlockSpec(memory_space=pltpu.VMEM),
+        out_specs=(pl.BlockSpec(memory_space=pltpu.VMEM),) * 2,
         compiler_params=SMALL,
     )(place, packed)
 
@@ -319,17 +333,19 @@
         for c in range(cols):
             partner = 2 * ((c // 2 + r // 4) % 8) + (r // 2 + c) % 2
             hop.append((r * cols + partner, r * cols + c))
+    place = jnp.stack([distance, side, odd]).astype(jnp.int32)
+    products, half = tile_products(place, packed)
+    partner = lax.ppermute(half, ("row", "col"), hop)
+    parts = lax.all_to_all(products, "col", 0, 0)
     own = packed[:, 64:, :].reshape(D // 2, BLK)
-    partner = lax.ppermute(own, ("row", "col"), hop)
-    place = jnp.stack([distance, side, odd]).astype(jnp.int32)
-    parts = lax.all_to_all(tile_products(place, packed), "col", 0, 0)
     own_norms = norms(own)
     own_norms = own_norms[:64] + own_norms[64:]
-    partner_norms = norms(partner)
-    partner_norms = partner_norms[:64] + partner_norms[64:]
-    inner = lax.dot_general(own, partner, (((0,), (0,)), ((), ())), preferred_element_type=f32)
-    tile = matern(inner[:64, :64] + inner[64:, 64:], own_norms, partner_norms)
-    tile = jnp.where(odd == 0, tile[:, :32], tile[:, 32:])
+    partner_norms = jnp.sum(norms(partner).reshape(4, 32), axis=0)
+    ends = (((0,), (0,)), ((), ()))
+    near = lax.dot_general(own[: D // 4], partner, ends, preferred_element_type=f32)
+    far = lax.dot_general(own[D // 4 :], partner, ends, preferred_element_type=f32)
+    inner = (near[:64, :32] + near[64:, 32:64]) + (far[:64, 64:96] + far[64:, 96:])
+    tile = matern(inner, own_norms, partner_norms)
     line = jnp.arange(64, dtype=jnp.int32)[:, None] - 32 * odd
     tile = tile + jnp.where(line == jnp.arange(32, dtype=jnp.int32)[None, :], own_noise[None, :], 0.0)
     tile = jnp.concatenate([tile[16 * q : 16 * q + 16] for q in range(4)], axis=1)

time: 196 us -> 187 us (0.954)
  starting transfers between devices: 57.3 us -> 47.9 us
    all_to_all x1, starting transfers between devices: 20.7 us -> 10.6 us  [body(): lax.all_to_all(sent, 'row', 0, 0)]
  transfers between devices with their start and end apart: 8 -> 8, of which waited for: 5 -> 5; matrix products, arithmetic and copies ran while one was open for 3% -> 4% of each run, Pallas kernels for 2% -> 2%
where the time goes in v4:
time: 187 us; the launch traced here: 186 us
  waiting for transfers between devices  50.5 us (27%)
  starting transfers between devices  47.9 us (26%)
  Pallas kernels  43.9 us (23%)
  blocking collectives  19.1 us (10%)
  between operations  14.3 us (8%)
  other arithmetic  4.81 us (3%)
  local copies, waits for them, and re-layouts  3.14 us (2%)
  matrix products  2.51 us (1%)
    pallas_call x1, Pallas kernels, chol_solve(): pl.pallas_call(kernel, out_shape=(jax.ShapeDtypeStruct((64, N), f32), jax...  40.2 us
    all_gather x1, blocking collectives, body(): rhs = lax.all_gather(rhs_tile, 'col', axis=0, tiled=True)  19.1 us
    all_to_all x1, waiting for transfers between devices, spread(): return lax.all_to_all(lax.optimization_barrier(copies), axis, 0, 0)  17.8 us
    all_to_all x1, starting transfers between devices, spread(): return lax.all_to_all(lax.optimization_barrier(copies), axis, 0, 0)  13.7 us
    all_to_all x1, starting transfers between devices, body(): parts = lax.all_to_all(products, 'col', 0, 0)  12.5 us
    all_to_all x1, waiting for transfers between devices, body(): lax.all_to_all(rhs_part.astype(bf16).reshape(cols, 64, BLK), 'col', 0, 0)  12.1 us
    all_to_all x1, starting transfers between devices, body(): lax.all_to_all(sent, 'row', 0, 0)  10.6 us
    all_to_all x1, waiting for transfers between devices, body(): lax.all_to_all(sent, 'row', 0, 0)  9.65 us
  transfers between devices with their start and end apart: 8, of which 5 were waited for; matrix products, arithmetic and copies ran while one was open for 4% of the time, Pallas kernels for 2%

profile of v4, /device:TPU:1, one launch (start us, length us, event | category | flops | bytes accessed | tf_op | source)
XLA Modules:
  0.0 186.2 jit_solution(11918368461559993976)
XLA Ops:
  7.2 0.8 copy.37
  8.0 0.8 convert_element_type.24
  8.9 1.0 broadcast_in_dim.10
  9.9 13.7 %all-to-all-start = ((bf16[32,104,128]{2,1,0:T(8,128)(2,1)}), bf16[32,104,128]{2,1,0:T(8,128)(2,1)S(1)}, u32[]{:S(2)}, u32[]{:S(2)}) async-start(bf16[32,104,128]{2,1,0:T(8,128)(2,1)} %broadcast_in_dim.10), calls=%async_computation | async-start | bytes 1703936 | tf_op jit(solution)/shard_map/all_to_all | solution.py:295
  23.7 1.3 collective-permute-start.1
  25.2 0.7 maximum_maximum_fusion
  26.1 17.8 %all-to-all-done.packed_ref = bf16[32,104,128]{2,1,0:T(8,128)(2,1)S(1)} async-done(((bf16[32,104,128]{2,1,0:T(8,128)(2,1)}), bf16[32,104,128]{2,1,0:T(8,128)(2,1)S(1)}, u32[]{:S(2)}, u32[]{:S(2)}) %all-to-all-start) | async-done | bytes 852000 | tf_op jit(solution)/shard_map/all_to_all | solution.py:295
  44.0 2.0 %shard_map.94 = (f32[16,16,128]{2,1,0:T(8,128)}, bf16[640,128]{1,0:T(8,128)(2,1)S(1)}) custom-call(s32[3]{0:T(128)S(1)} %pad_add_fusion.place_ref, bf16[32,104,128]{2,1,0:T(8,128)(2,1)S(1)} %all-to-all-done.packed_ref), custom_call_target="tpu_custom_call" | custom-call | tf_op jit(solution)/shard_map/pallas_call | solution.py:264
  46.0 0.7 collective-permute-start
  46.7 12.5 %all-to-all-start.1 = ((f32[16,16,128]{2,1,0:T(8,128)}), f32[16,16,128]{2,1,0:T(8,128)S(1)}, u32[]{:S(2)}, u32[]{:S(2)}) async-start(f32[16,16,128]{2,1,0:T(8,128)} %get-tuple-element.7), calls=%async_computation.1 | async-start | bytes 262144 | tf_op jit(solution)/shard_map/all_to_all | solution.py:339
  59.2 0.2 multiply_reduce_fusion.1
  59.6 0.2 fusion.22
  59.9 0.2 fusion.23
  60.2 0.1 select_add_fusion
  60.4 8.0 %all-to-all-done.1.parts_ref = f32[16,16,128]{2,1,0:T(8,128)S(1)} async-done(((f32[16,16,128]{2,1,0:T(8,128)}), f32[16,16,128]{2,1,0:T(8,128)S(1)}, u32[]{:S(2)}, u32[]{:S(2)}) %all-to-all-start.1) | async-done | bytes 131104 | tf_op jit(solution)/shard_map/all_to_all | solution.py:339
  68.4 0.7 shard_map.95
  69.1 10.6 %all-to-all-start.2 = ((f32[32,16,128]{2,1,0:T(8,128)}), f32[32,16,128]{2,1,0:T(8,128)S(1)}, u32[]{:S(2)}, u32[]{:S(2)}) async-start(f32[32,16,128]{2,1,0:T(8,128)} %shard_map.95), calls=%async_computation.2 | async-start | bytes 524288 | tf_op jit(solution)/shard_map/all_to_all | solution.py:353
  79.8 9.7 %all-to-all-done.2.tiles_ref = f32[32,16,128]{2,1,0:T(8,128)S(1)} async-done(((f32[32,16,128]{2,1,0:T(8,128)}), f32[32,16,128]{2,1,0:T(8,128)S(1)}, u32[]{:S(2)}, u32[]{:S(2)}) %all-to-all-start.2) | async-done | bytes 262176 | tf_op jit(solution)/shard_map/all_to_all | solution.py:353
  89.4 1.0 shard_map.96
  90.5 0.7 copy-done
  91.2 0.3 convolution_convert_fusion
  91.5 0.3 convolution_convert_fusion.1
  91.8 0.9 pad_maximum_fusion.2
  92.7 9.1 %all-to-all-start.3 = ((bf16[16,64,128]{2,1,0:T(8,128)(2,1)}), bf16[16,64,128]{2,1,0:T(8,128)(2,1)S(1)}, u32[]{:S(2)}, u32[]{:S(2)}) async-start(bf16[16,64,128]{2,1,0:T(8,128)(2,1)} %pad_maximum_fusion.2), calls=%async_computation.3 | async-start | bytes 524288 | tf_op jit(solution)/shard_map/all_to_all | solution.py:361
  101.7 0.2 slice_bitcast_fusion.1
  101.9 0.1 pad_maximum_fusion
  102.2 1.4 multiply_reduce_fusion
  103.6 12.1 %all-to-all-done.3 = bf16[16,64,128]{2,1,0:T(8,128)(2,1)S(1)} async-done(((bf16[16,64,128]{2,1,0:T(8,128)(2,1)}), bf16[16,64,128]{2,1,0:T(8,128)(2,1)S(1)}, u32[]{:S(2)}, u32[]{:S(2)}) %all-to-all-start.3) | async-done | bytes 262176 | tf_op jit(solution)/shard_map/all_to_all | solution.py:361
  115.7 1.5 multiply_subtract_fusion
  117.2 19.1 %all_gather.11.rhs_ref = f32[1024,128]{1,0:T(8,128)} all-gather(f32[64,128]{1,0:T(8,128)S(1)} %multiply_subtract_fusion), channel_id=1, replica_groups=mesh['row'=32,'col'=16] {'col'}, dimensions={0}, use_global_device_ids=true | all-gather | bytes 557056 | tf_op jit(solution)/shard_map/all_gather | solution.py:367
  136.3 2.8 %all-gather.3.cloned.1.call-done.a_ref = f32[1024,1024]{1,0:T(8,128)} async-done(((f32[64,1024]{1,0:T(8,128)}), f32[1024,1024]{1,0:T(8,128)}) %all-gather.3.cloned.1.call-update) | async-done | bytes 4194320 | tf_op jit(solution)/shard_map/all_gather | solution.py:355
  139.1 40.2 %shard_map.97 = (f32[64,1024]{1,0:T(8,128)}, f32[64,64]{1,0:T(8,128)}, f32[64,64]{1,0:T(8,128)}) custom-call(s32[1]{0:T(128)} %bitcast.c_ref, f32[1024,1024]{1,0:T(8,128)} %all-gather.3.cloned.1.call-done.a_ref, f32[1024,128]{1,0:T(8,128)} %all_gather.11.rhs_ref), custom_call_target="tpu_custom_call" | custom-call | flops 3000000000 | bytes 5000000 | tf_op jit(solution)/shard_map/pallas_call | solution.py:179
  (36 shorter events, 1.2 us)
Async XLA Ops:
  8.8 14.9 %copy-start.4 = (f32[32]{0:T(128)S(1)}, f32[32]{0:T(128)}, u32[]{:S(2)}) copy-start(f32[32]{0:T(128)} %param.13) | copy-start | bytes 388
  8.8 16.2 %copy-start.2 = (bf16[64,160]{1,0:T(8,128)(2,1)S(1)}, bf16[64,160]{1,0:T(8,128)(2,1)}, u32[]{:S(2)}) copy-start(bf16[64,160]{1,0:T(8,128)(2,1)} %param.7) | copy-start | bytes 61444
  8.9 16.2 %copy-start.3 = (bf16[64,160]{1,0:T(8,128)(2,1)S(1)}, bf16[64,160]{1,0:T(8,128)(2,1)}, u32[]{:S(2)}) copy-start(bf16[64,160]{1,0:T(8,128)(2,1)} %param.9) | copy-start | bytes 61444
  9.9 34.1 %all-to-all-start = ((bf16[32,104,128]{2,1,0:T(8,128)(2,1)}), bf16[32,104,128]{2,1,0:T(8,128)(2,1)S(1)}, u32[]{:S(2)}, u32[]{:S(2)}) async-start(bf16[32,104,128]{2,1,0:T(8,128)(2,1)} %broadcast_in_dim.10), calls=%async_computation | async-start | bytes 1703936 | tf_op jit(solution)/shard_map/all_to_all | solution.py:295
  23.6 78.5 %all-gather.5.cloned.1.call-start = ((), (), s32[]{:S(2)}) async-start(), calls=%async_computation.5 | async-start | bytes 1392640 | tf_op jit(solution)/shard_map/all_gather | solution.py:320
  23.7 36.5 %collective-permute-start.1 = (f32[32]{0:T(128)S(1)}, f32[32]{0:T(128)S(1)}, u32[]{:S(2)}, u32[]{:S(2)}) collective-permute-start(f32[32]{0:T(128)S(1)} %copy-done.4), channel_id=1, source_target_pairs={{0,0},{16,16},{33,1},{49,17},{66,2},{82,18},{99,3},{115,19},{132,4... | collective-permute-start | bytes 392 | tf_op jit(solution)/shard_map/ppermute | solution.py:330
  46.0 13.5 %collective-permute-start = (bf16[640,128]{1,0:T(8,128)(2,1)S(1)}, bf16[640,128]{1,0:T(8,128)(2,1)S(1)}, u32[]{:S(2)}, u32[]{:S(2)}) collective-permute-start(bf16[640,128]{1,0:T(8,128)(2,1)S(1)} %get-tuple-element.8), channel_id=1, source_target_pairs={{0,0},{1,1},{2,2},{3,3},{4,4},{5,5},{6,6},{7,7},{8,8},{9,9},{10,10... | collective-permute-start | bytes 491528 | tf_op jit(solution)/shard_map/ppermute | solution.py:338
  46.7 21.7 %all-to-all-start.1 = ((f32[16,16,128]{2,1,0:T(8,128)}), f32[16,16,128]{2,1,0:T(8,128)S(1)}, u32[]{:S(2)}, u32[]{:S(2)}) async-start(f32[16,16,128]{2,1,0:T(8,128)} %get-tuple-element.7), calls=%async_computation.1 | async-start | bytes 262144 | tf_op jit(solution)/shard_map/all_to_all | solution.py:339
  69.1 20.3 %all-to-all-start.2 = ((f32[32,16,128]{2,1,0:T(8,128)}), f32[32,16,128]{2,1,0:T(8,128)S(1)}, u32[]{:S(2)}, u32[]{:S(2)}) async-start(f32[32,16,128]{2,1,0:T(8,128)} %shard_map.95), calls=%async_computation.2 | async-start | bytes 524288 | tf_op jit(solution)/shard_map/all_to_all | solution.py:353
  79.7 59.4 %all-gather.3.cloned.1.call-start = ((), (), s32[]{:S(2)}) async-start(), calls=%async_computation.4 | async-start | bytes 4456448 | tf_op jit(solution)/shard_map/all_gather | solution.py:355
  90.4 0.8 copy-start
  90.4 1.1 copy-start.1
  92.7 23.0 %all-to-all-start.3 = ((bf16[16,64,128]{2,1,0:T(8,128)(2,1)}), bf16[16,64,128]{2,1,0:T(8,128)(2,1)S(1)}, u32[]{:S(2)}, u32[]{:S(2)}) async-start(bf16[16,64,128]{2,1,0:T(8,128)(2,1)} %pad_maximum_fusion.2), calls=%async_computation.3 | async-start | bytes 524288 | tf_op jit(solution)/shard_map/all_to_all | solution.py:361
Sparse Core Ops, SparseCore 0:
  26.6 43.5 all-gather.4
  90.5 48.5 all-gather.2

commit v5 on v4

--- a/solution.py
+++ b/solution.py
@@ -1,5 +1,3 @@
-import functools
-
 import jax
 import jax.numpy as jnp
 from jax import lax
@@ -117,15 +115,22 @@
     panel = mm(left(t[start:, i * BLK : start]), inverse, True)
     pa[start:, :] = left(panel)
     pb[start:, :] = right(panel)
+    t[start:, start : start + BLK] -= mm(pa[start:, :], pb[start : start + BLK, :], True)
+
+
+def rest(i, t, rt, pa, pb, solved):
+    start = (i + 1) * BLK
+    if start == N:
+        return
     rt[start:, :] -= mm(pa[start:, :], solved)
-    first = start
+    first = start + BLK
     while first < N:
         wide = 256 if (N - first) % 256 == 0 else 128
         t[first:, first : first + wide] -= mm(pa[first:, :], pb[first : first + wide, :], True)
         first += wide
 
 
-def kernel(c_ref, a_ref, rhs_ref, diag_ref, panel_ref, cand_ref, t, rt, linv, pa, pb, sems):
+def kernel(c_ref, a_ref, rhs_ref, diag_ref, panel_ref, cand_ref, t, rt, pa, pb, sems):
     copies = []
     for k in range(8):
         rows = pl.ds(k * BLK, BLK)
@@ -143,34 +148,27 @@
     mine = pl.multiple_of(c_ref[0] * 64, 64)
     rt[...] = rhs_ref[...]
     copies[0].wait()
-
-    def step(kb, _):
-        base = pl.multiple_of(kb * BLK, BLK)
-        D = [t[pl.ds(pl.multiple_of(base + 8 * v, 8), 8), pl.ds(base, BLK)] for v in range(16)]
-
-        def store(g, rows):
-            linv[8 * g : 8 * g + 8, :] = rows
-
-        factor_inverse(D, store)
-
-        @pl.when(kb == 0)
-        def _():
+    ri = lax.broadcasted_iota(jnp.int32, (64, BLK), 0) + mine
+    ci = lax.broadcasted_iota(jnp.int32, (64, BLK), 1)
+    before = None
+    for kb in range(8):
+        base = kb * BLK
+        D = [t[base + 8 * v : base + 8 * v + 8, base : base + BLK] for v in range(16)]
+        slabs = []
+        factor_inverse(D, lambda g, rows, slabs=slabs: slabs.append(rows))
+        if before is not None:
+            rest(kb - 1, t, rt, pa.at[(kb - 1) % 2], pb.at[(kb - 1) % 2], before)
+        low_inverse = jnp.concatenate(slabs, axis=0)
+        if kb == 0:
             for copy in copies[1:]:
                 copy.wait()
-
-        inverse = right(linv[...])
-        low = mm(left(t[pl.ds(mine, 64), pl.ds(base, BLK)]), inverse, True)
-        ri = lax.broadcasted_iota(jnp.int32, (64, BLK), 0) + mine
-        ci = lax.broadcasted_iota(jnp.int32, (64, BLK), 1) + base
-        diag_ref[:, pl.ds(base, BLK)] = jnp.where(ri >= ci, low, 0.0)
-        solved = mm(left(linv[...]), right(rt[pl.ds(base, BLK), :], 0))
-        rt[pl.ds(base, BLK), :] = solved
-        solved = right(solved, 0)
-        for i in range(8):
-            pl.when(kb == i)(functools.partial(eliminate, i, t, rt, pa, pb, inverse, solved))
-        return 0
-
-    lax.fori_loop(0, 8, step, 0)
+        inverse = right(low_inverse)
+        low = mm(left(t[pl.ds(mine, 64), base : base + BLK]), inverse, True)
+        diag_ref[:, base : base + BLK] = jnp.where(ri >= ci + base, low, 0.0)
+        solved = mm(left(low_inverse), right(rt[base : base + BLK, :], 0))
+        rt[base : base + BLK, :] = solved
+        before = right(solved, 0)
+        eliminate(kb, t, rt, pa.at[kb % 2], pb.at[kb % 2], inverse, before)
     panel_ref[...] = rt[pl.ds(mine, 64), :64]
     cand_ref[...] = rt[pl.ds(mine, 64), 64:]
 
@@ -192,9 +190,8 @@
         scratch_shapes=[
             pltpu.VMEM((N, N), f32),
             pltpu.VMEM((N, BLK), f32),
-            pltpu.VMEM((BLK, BLK), f32),
-            pltpu.VMEM((N, 3 * BLK), bf16),
-            pltpu.VMEM((N, 3 * BLK), bf16),
+            pltpu.VMEM((2, N, 3 * BLK), bf16),
+            pltpu.VMEM((2, N, 3 * BLK), bf16),
             pltpu.SemaphoreType.DMA((15,)),
         ],
         compiler_params=pltpu.CompilerParams(vmem_limit_bytes=60 * 1024 * 1024),

time: 187 us -> 182 us (0.973)
  Pallas kernels: 43.9 us -> 39.2 us
    pallas_call x1, Pallas kernels: 40.2 us -> 35.5 us  [chol_solve(): pl.pallas_call(kernel, out_shape=(jax.ShapeDtypeStruct((64, N), f32), jax...]
where the time goes in v5:
time: 182 us; the launch traced here: 181 us
  waiting for transfers between devices  50.5 us (28%)
  starting transfers between devices  47.9 us (26%)
  Pallas kernels  39.2 us (22%)
  blocking collectives  19.1 us (10%)
  between operations  14.3 us (8%)
  other arithmetic  4.81 us (3%)
  local copies, waits for them, and re-layouts  3.14 us (2%)
  matrix products  2.51 us (1%)
    pallas_call x1, Pallas kernels, chol_solve(): pl.pallas_call(kernel, out_shape=(jax.ShapeDtypeStruct((64, N), f32), jax...  35.5 us
    all_gather x1, blocking collectives, body(): rhs = lax.all_gather(rhs_tile, 'col', axis=0, tiled=True)  19.1 us
    all_to_all x1, waiting for transfers between devices, spread(): return lax.all_to_all(lax.optimization_barrier(copies), axis, 0, 0)  17.8 us
    all_to_all x1, starting transfers between devices, spread(): return lax.all_to_all(lax.optimization_barrier(copies), axis, 0, 0)  13.7 us
    all_to_all x1, starting transfers between devices, body(): parts = lax.all_to_all(products, 'col', 0, 0)  12.5 us
    all_to_all x1, waiting for transfers between devices, body(): lax.all_to_all(rhs_part.astype(bf16).reshape(cols, 64, BLK), 'col', 0, 0)  12.1 us
    all_to_all x1, starting transfers between devices, body(): lax.all_to_all(sent, 'row', 0, 0)  10.6 us
    all_to_all x1, waiting for transfers between devices, body(): lax.all_to_all(sent, 'row', 0, 0)  9.65 us
  transfers between devices with their start and end apart: 8, of which 5 were waited for; matrix products, arithmetic and copies ran while one was open for 4% of the time, Pallas kernels for 2%

profile of v5, /device:TPU:1, one launch (start us, length us, event | category | flops | bytes accessed | tf_op | source)
XLA Modules:
  0.0 181.4 jit_solution(5310169715608033054)
XLA Ops:
  7.2 0.8 copy.37
  8.0 0.8 convert_element_type.24
  8.9 1.0 broadcast_in_dim.10
  9.9 13.7 %all-to-all-start = ((bf16[32,104,128]{2,1,0:T(8,128)(2,1)}), bf16[32,104,128]{2,1,0:T(8,128)(2,1)S(1)}, u32[]{:S(2)}, u32[]{:S(2)}) async-start(bf16[32,104,128]{2,1,0:T(8,128)(2,1)} %broadcast_in_dim.10), calls=%async_computation | async-start | bytes 1703936 | tf_op jit(solution)/shard_map/all_to_all | solution.py:292
  23.7 1.3 collective-permute-start.1
  25.2 0.7 maximum_maximum_fusion
  26.1 17.8 %all-to-all-done.packed_ref = bf16[32,104,128]{2,1,0:T(8,128)(2,1)S(1)} async-done(((bf16[32,104,128]{2,1,0:T(8,128)(2,1)}), bf16[32,104,128]{2,1,0:T(8,128)(2,1)S(1)}, u32[]{:S(2)}, u32[]{:S(2)}) %all-to-all-start) | async-done | bytes 852000 | tf_op jit(solution)/shard_map/all_to_all | solution.py:292
  44.0 2.0 %shard_map.94 = (f32[16,16,128]{2,1,0:T(8,128)}, bf16[640,128]{1,0:T(8,128)(2,1)S(1)}) custom-call(s32[3]{0:T(128)S(1)} %pad_add_fusion.place_ref, bf16[32,104,128]{2,1,0:T(8,128)(2,1)S(1)} %all-to-all-done.packed_ref), custom_call_target="tpu_custom_call" | custom-call | tf_op jit(solution)/shard_map/pallas_call | solution.py:261
  46.0 0.7 collective-permute-start
  46.7 12.5 %all-to-all-start.1 = ((f32[16,16,128]{2,1,0:T(8,128)}), f32[16,16,128]{2,1,0:T(8,128)S(1)}, u32[]{:S(2)}, u32[]{:S(2)}) async-start(f32[16,16,128]{2,1,0:T(8,128)} %get-tuple-element.7), calls=%async_computation.1 | async-start | bytes 262144 | tf_op jit(solution)/shard_map/all_to_all | solution.py:336
  59.2 0.2 multiply_reduce_fusion.1
  59.6 0.2 fusion.22
  59.9 0.2 fusion.23
  60.2 0.1 select_add_fusion
  60.4 8.0 %all-to-all-done.1.parts_ref = f32[16,16,128]{2,1,0:T(8,128)S(1)} async-done(((f32[16,16,128]{2,1,0:T(8,128)}), f32[16,16,128]{2,1,0:T(8,128)S(1)}, u32[]{:S(2)}, u32[]{:S(2)}) %all-to-all-start.1) | async-done | bytes 131104 | tf_op jit(solution)/shard_map/all_to_all | solution.py:336
  68.4 0.7 shard_map.95
  69.1 10.6 %all-to-all-start.2 = ((f32[32,16,128]{2,1,0:T(8,128)}), f32[32,16,128]{2,1,0:T(8,128)S(1)}, u32[]{:S(2)}, u32[]{:S(2)}) async-start(f32[32,16,128]{2,1,0:T(8,128)} %shard_map.95), calls=%async_computation.2 | async-start | bytes 524288 | tf_op jit(solution)/shard_map/all_to_all | solution.py:350
  79.8 9.7 %all-to-all-done.2.tiles_ref = f32[32,16,128]{2,1,0:T(8,128)S(1)} async-done(((f32[32,16,128]{2,1,0:T(8,128)}), f32[32,16,128]{2,1,0:T(8,128)S(1)}, u32[]{:S(2)}, u32[]{:S(2)}) %all-to-all-start.2) | async-done | bytes 262176 | tf_op jit(solution)/shard_map/all_to_all | solution.py:350
  89.4 1.0 shard_map.96
  90.5 0.7 copy-done
  91.2 0.3 convolution_convert_fusion
  91.5 0.3 convolution_convert_fusion.1
  91.8 0.9 pad_maximum_fusion.2
  92.7 9.1 %all-to-all-start.3 = ((bf16[16,64,128]{2,1,0:T(8,128)(2,1)}), bf16[16,64,128]{2,1,0:T(8,128)(2,1)S(1)}, u32[]{:S(2)}, u32[]{:S(2)}) async-start(bf16[16,64,128]{2,1,0:T(8,128)(2,1)} %pad_maximum_fusion.2), calls=%async_computation.3 | async-start | bytes 524288 | tf_op jit(solution)/shard_map/all_to_all | solution.py:358
  101.7 0.2 slice_bitcast_fusion.1
  101.9 0.1 pad_maximum_fusion
  102.2 1.4 multiply_reduce_fusion
  103.6 12.1 %all-to-all-done.3 = bf16[16,64,128]{2,1,0:T(8,128)(2,1)S(1)} async-done(((bf16[16,64,128]{2,1,0:T(8,128)(2,1)}), bf16[16,64,128]{2,1,0:T(8,128)(2,1)S(1)}, u32[]{:S(2)}, u32[]{:S(2)}) %all-to-all-start.3) | async-done | bytes 262176 | tf_op jit(solution)/shard_map/all_to_all | solution.py:358
  115.7 1.5 multiply_subtract_fusion
  117.2 19.1 %all_gather.11.rhs_ref = f32[1024,128]{1,0:T(8,128)} all-gather(f32[64,128]{1,0:T(8,128)S(1)} %multiply_subtract_fusion), channel_id=1, replica_groups=mesh['row'=32,'col'=16] {'col'}, dimensions={0}, use_global_device_ids=true | all-gather | bytes 557056 | tf_op jit(solution)/shard_map/all_gather | solution.py:364
  136.3 2.8 %all-gather.3.cloned.1.call-done.a_ref = f32[1024,1024]{1,0:T(8,128)} async-done(((f32[64,1024]{1,0:T(8,128)}), f32[1024,1024]{1,0:T(8,128)}) %all-gather.3.cloned.1.call-update) | async-done | bytes 4194320 | tf_op jit(solution)/shard_map/all_gather | solution.py:352
  139.1 35.5 %shard_map.97 = (f32[64,1024]{1,0:T(8,128)}, f32[64,64]{1,0:T(8,128)}, f32[64,64]{1,0:T(8,128)}) custom-call(s32[1]{0:T(128)} %bitcast.c_ref, f32[1024,1024]{1,0:T(8,128)} %all-gather.3.cloned.1.call-done.a_ref, f32[1024,128]{1,0:T(8,128)} %all_gather.11.rhs_ref), custom_call_target="tpu_custom_call" | custom-call | flops 3000000000 | bytes 5000000 | tf_op jit(solution)/shard_map/pallas_call | solution.py:177
  (36 shorter events, 1.2 us)
Async XLA Ops:
  8.8 14.9 %copy-start.4 = (f32[32]{0:T(128)S(1)}, f32[32]{0:T(128)}, u32[]{:S(2)}) copy-start(f32[32]{0:T(128)} %param.13) | copy-start | bytes 388
  8.8 16.2 %copy-start.2 = (bf16[64,160]{1,0:T(8,128)(2,1)S(1)}, bf16[64,160]{1,0:T(8,128)(2,1)}, u32[]{:S(2)}) copy-start(bf16[64,160]{1,0:T(8,128)(2,1)} %param.7) | copy-start | bytes 61444
  8.9 16.2 %copy-start.3 = (bf16[64,160]{1,0:T(8,128)(2,1)S(1)}, bf16[64,160]{1,0:T(8,128)(2,1)}, u32[]{:S(2)}) copy-start(bf16[64,160]{1,0:T(8,128)(2,1)} %param.9) | copy-start | bytes 61444
  9.9 34.1 %all-to-all-start = ((bf16[32,104,128]{2,1,0:T(8,128)(2,1)}), bf16[32,104,128]{2,1,0:T(8,128)(2,1)S(1)}, u32[]{:S(2)}, u32[]{:S(2)}) async-start(bf16[32,104,128]{2,1,0:T(8,128)(2,1)} %broadcast_in_dim.10), calls=%async_computation | async-start | bytes 1703936 | tf_op jit(solution)/shard_map/all_to_all | solution.py:292
  23.6 78.5 %all-gather.5.cloned.1.call-start = ((), (), s32[]{:S(2)}) async-start(), calls=%async_computation.5 | async-start | bytes 1392640 | tf_op jit(solution)/shard_map/all_gather | solution.py:317
  23.7 36.5 %collective-permute-start.1 = (f32[32]{0:T(128)S(1)}, f32[32]{0:T(128)S(1)}, u32[]{:S(2)}, u32[]{:S(2)}) collective-permute-start(f32[32]{0:T(128)S(1)} %copy-done.4), channel_id=1, source_target_pairs={{0,0},{16,16},{33,1},{49,17},{66,2},{82,18},{99,3},{115,19},{132,4... | collective-permute-start | bytes 392 | tf_op jit(solution)/shard_map/ppermute | solution.py:327
  46.0 13.5 %collective-permute-start = (bf16[640,128]{1,0:T(8,128)(2,1)S(1)}, bf16[640,128]{1,0:T(8,128)(2,1)S(1)}, u32[]{:S(2)}, u32[]{:S(2)}) collective-permute-start(bf16[640,128]{1,0:T(8,128)(2,1)S(1)} %get-tuple-element.8), channel_id=1, source_target_pairs={{0,0},{1,1},{2,2},{3,3},{4,4},{5,5},{6,6},{7,7},{8,8},{9,9},{10,10... | collective-permute-start | bytes 491528 | tf_op jit(solution)/shard_map/ppermute | solution.py:335
  46.7 21.7 %all-to-all-start.1 = ((f32[16,16,128]{2,1,0:T(8,128)}), f32[16,16,128]{2,1,0:T(8,128)S(1)}, u32[]{:S(2)}, u32[]{:S(2)}) async-start(f32[16,16,128]{2,1,0:T(8,128)} %get-tuple-element.7), calls=%async_computation.1 | async-start | bytes 262144 | tf_op jit(solution)/shard_map/all_to_all | solution.py:336
  69.1 20.3 %all-to-all-start.2 = ((f32[32,16,128]{2,1,0:T(8,128)}), f32[32,16,128]{2,1,0:T(8,128)S(1)}, u32[]{:S(2)}, u32[]{:S(2)}) async-start(f32[32,16,128]{2,1,0:T(8,128)} %shard_map.95), calls=%async_computation.2 | async-start | bytes 524288 | tf_op jit(solution)/shard_map/all_to_all | solution.py:350
  79.7 59.4 %all-gather.3.cloned.1.call-start = ((), (), s32[]{:S(2)}) async-start(), calls=%async_computation.4 | async-start | bytes 4456448 | tf_op jit(solution)/shard_map/all_gather | solution.py:352
  90.4 0.8 copy-start
  90.4 1.1 copy-start.1
  92.7 23.0 %all-to-all-start.3 = ((bf16[16,64,128]{2,1,0:T(8,128)(2,1)}), bf16[16,64,128]{2,1,0:T(8,128)(2,1)S(1)}, u32[]{:S(2)}, u32[]{:S(2)}) async-start(bf16[16,64,128]{2,1,0:T(8,128)(2,1)} %pad_maximum_fusion.2), calls=%async_computation.3 | async-start | bytes 524288 | tf_op jit(solution)/shard_map/all_to_all | solution.py:358
Sparse Core Ops, SparseCore 0:
  26.6 43.5 all-gather.4
  90.5 48.5 all-gather.2

commit v6 on v5

--- a/solution.py
+++ b/solution.py
@@ -202,6 +202,26 @@
 SMALL = pltpu.CompilerParams(vmem_limit_bytes=8 * 1024 * 1024)
 
 
+def pack_kernel(factor_ref, points_ref, out_ref):
+    factor = factor_ref[...].astype(bf16)
+    points = points_ref[...].astype(f32).T
+    points = jnp.concatenate([points[:40], points[40:]], axis=1).astype(bf16)
+    for r in range(32):
+        out_ref[r, :32, :] = factor[:, :BLK]
+        out_ref[r, 32:64, :] = factor[:, BLK:]
+        out_ref[r, 64:, :] = points
+
+
+def pack_copies(factor, points):
+    return pl.pallas_call(
+        pack_kernel,
+        out_shape=jax.ShapeDtypeStruct((32, 104, BLK), bf16),
+        in_specs=[pl.BlockSpec(memory_space=pltpu.VMEM)] * 2,
+        out_specs=pl.BlockSpec(memory_space=pltpu.VMEM),
+        compiler_params=SMALL,
+    )(factor, points)
+
+
 def slab_kernel(c_ref, tiles_ref, out_ref):
     swap = c_ref[0] % 2
     place = lax.broadcasted_iota(jnp.int32, (16, BLK), 1) // 32
@@ -287,11 +307,6 @@
     )(parts, tile)
 
 
-def spread(value, axis, count):
-    copies = jnp.broadcast_to(value[None], (count,) + value.shape)
-    return lax.all_to_all(lax.optimization_barrier(copies), axis, 0, 0)
-
-
 def matern(inner, left_norms, right_norms):
     squared = jnp.maximum(left_norms[:, None] + right_norms[None, :] - 2.0 * inner, 0.0)
     scaled = jnp.sqrt(5.0 * squared / D)
@@ -317,12 +332,7 @@
     points_t = lax.all_gather(
         jnp.concatenate([trail_points.T, cand_points.T, pad], axis=1), "col", axis=0, tiled=True
     )
-    block_t = block_points.T
-    flat = block_factor.astype(bf16)
-    packed = jnp.concatenate(
-        [flat[:, :BLK], flat[:, BLK:], jnp.concatenate([block_t[:40], block_t[40:]], axis=1)], axis=0
-    )
-    packed = spread(packed, "row", rows)
+    packed = lax.all_to_all(pack_copies(block_factor, block_points), "row", 0, 0)
     settle = [((2 * c + h) * cols + c, h * cols + c) for c in range(cols) for h in range(2)]
     own_noise = lax.ppermute(noise, ("row", "col"), settle)
     hop = []

time: 182 us -> 182 us (level)
  no operation moved by 1% of the time
where the time goes in v6:
time: 182 us; the launch traced here: 181 us
  waiting for transfers between devices  50.5 us (28%)
  starting transfers between devices  47.9 us (26%)
  Pallas kernels  40.3 us (22%)
  blocking collectives  19 us (10%)
  between operations  14.3 us (8%)
  other arithmetic  3.97 us (2%)
  local copies, waits for them, and re-layouts  2.76 us (2%)
  matrix products  2.51 us (1%)
    pallas_call x1, Pallas kernels, chol_solve(): pl.pallas_call(kernel, out_shape=(jax.ShapeDtypeStruct((64, N), f32), jax...  35.4 us
    all_gather x1, blocking collectives, body(): rhs = lax.all_gather(rhs_tile, 'col', axis=0, tiled=True)  19 us
    all_to_all x1, waiting for transfers between devices, body(): lax.all_to_all(pack_copies(block_factor, block_points), 'row', 0, 0)  17.8 us
    all_to_all x1, starting transfers between devices, body(): lax.all_to_all(pack_copies(block_factor, block_points), 'row', 0, 0)  13.7 us
    all_to_all x1, starting transfers between devices, body(): parts = lax.all_to_all(products, 'col', 0, 0)  12.5 us
    all_to_all x1, waiting for transfers between devices, body(): lax.all_to_all(rhs_part.astype(bf16).reshape(cols, 64, BLK), 'col', 0, 0)  12.1 us
    all_to_all x1, starting transfers between devices, body(): lax.all_to_all(sent, 'row', 0, 0)  10.6 us
    all_to_all x1, waiting for transfers between devices, body(): lax.all_to_all(sent, 'row', 0, 0)  9.65 us
  transfers between devices with their start and end apart: 8, of which 5 were waited for; matrix products, arithmetic and copies ran while one was open for 4% of the time, Pallas kernels for 2%

profile of v6, /device:TPU:1, one launch (start us, length us, event | category | flops | bytes accessed | tf_op | source)
XLA Modules:
  0.0 181.2 jit_solution(159907155882609022)
XLA Ops:
  7.2 0.7 copy-done
  7.9 0.7 copy-done.1
  8.6 1.1 shard_map.94
  9.7 13.7 %all-to-all-start = ((bf16[32,104,128]{2,1,0:T(8,128)(2,1)}), bf16[32,104,128]{2,1,0:T(8,128)(2,1)S(1)}, u32[]{:S(2)}, u32[]{:S(2)}) async-start(bf16[32,104,128]{2,1,0:T(8,128)(2,1)} %shard_map.94), calls=%async_computation | async-start | bytes 1703936 | tf_op jit(solution)/shard_map/all_to_all | solution.py:335
  23.5 1.3 collective-permute-start.1
  25.1 0.7 maximum_maximum_fusion
  26.0 17.8 %all-to-all-done.packed_ref = bf16[32,104,128]{2,1,0:T(8,128)(2,1)S(1)} async-done(((bf16[32,104,128]{2,1,0:T(8,128)(2,1)}), bf16[32,104,128]{2,1,0:T(8,128)(2,1)S(1)}, u32[]{:S(2)}, u32[]{:S(2)}) %all-to-all-start) | async-done | bytes 852000 | tf_op jit(solution)/shard_map/all_to_all | solution.py:335
  43.8 2.0 %shard_map.95 = (f32[16,16,128]{2,1,0:T(8,128)}, bf16[640,128]{1,0:T(8,128)(2,1)S(1)}) custom-call(s32[3]{0:T(128)S(1)} %pad_add_fusion.place_ref, bf16[32,104,128]{2,1,0:T(8,128)(2,1)S(1)} %all-to-all-done.packed_ref), custom_call_target="tpu_custom_call" | custom-call | tf_op jit(solution)/shard_map/pallas_call | solution.py:281
  45.8 0.7 collective-permute-start
  46.5 12.5 %all-to-all-start.1 = ((f32[16,16,128]{2,1,0:T(8,128)}), f32[16,16,128]{2,1,0:T(8,128)S(1)}, u32[]{:S(2)}, u32[]{:S(2)}) async-start(f32[16,16,128]{2,1,0:T(8,128)} %get-tuple-element.7), calls=%async_computation.1 | async-start | bytes 262144 | tf_op jit(solution)/shard_map/all_to_all | solution.py:346
  59.0 0.2 multiply_reduce_fusion.1
  59.5 0.2 fusion.20
  59.7 0.2 fusion.21
  60.0 0.1 select_add_fusion
  60.2 8.0 %all-to-all-done.1.parts_ref = f32[16,16,128]{2,1,0:T(8,128)S(1)} async-done(((f32[16,16,128]{2,1,0:T(8,128)}), f32[16,16,128]{2,1,0:T(8,128)S(1)}, u32[]{:S(2)}, u32[]{:S(2)}) %all-to-all-start.1) | async-done | bytes 131104 | tf_op jit(solution)/shard_map/all_to_all | solution.py:346
  68.3 0.7 shard_map.96
  69.0 10.6 %all-to-all-start.2 = ((f32[32,16,128]{2,1,0:T(8,128)}), f32[32,16,128]{2,1,0:T(8,128)S(1)}, u32[]{:S(2)}, u32[]{:S(2)}) async-start(f32[32,16,128]{2,1,0:T(8,128)} %shard_map.96), calls=%async_computation.2 | async-start | bytes 524288 | tf_op jit(solution)/shard_map/all_to_all | solution.py:360
  79.6 9.7 %all-to-all-done.2.tiles_ref = f32[32,16,128]{2,1,0:T(8,128)S(1)} async-done(((f32[32,16,128]{2,1,0:T(8,128)}), f32[32,16,128]{2,1,0:T(8,128)S(1)}, u32[]{:S(2)}, u32[]{:S(2)}) %all-to-all-start.2) | async-done | bytes 262176 | tf_op jit(solution)/shard_map/all_to_all | solution.py:360
  89.3 1.0 shard_map.97
  90.4 0.7 copy-done.2
  91.1 0.3 convolution_convert_fusion
  91.4 0.3 convolution_convert_fusion.1
  91.7 0.9 pad_maximum_fusion.2
  92.5 9.1 %all-to-all-start.3 = ((bf16[16,64,128]{2,1,0:T(8,128)(2,1)}), bf16[16,64,128]{2,1,0:T(8,128)(2,1)S(1)}, u32[]{:S(2)}, u32[]{:S(2)}) async-start(bf16[16,64,128]{2,1,0:T(8,128)(2,1)} %pad_maximum_fusion.2), calls=%async_computation.3 | async-start | bytes 524288 | tf_op jit(solution)/shard_map/all_to_all | solution.py:368
  101.6 0.2 slice_bitcast_fusion.1
  101.7 0.1 pad_maximum_fusion
  102.0 1.4 multiply_reduce_fusion
  103.4 12.1 %all-to-all-done.3 = bf16[16,64,128]{2,1,0:T(8,128)(2,1)S(1)} async-done(((bf16[16,64,128]{2,1,0:T(8,128)(2,1)}), bf16[16,64,128]{2,1,0:T(8,128)(2,1)S(1)}, u32[]{:S(2)}, u32[]{:S(2)}) %all-to-all-start.3) | async-done | bytes 262176 | tf_op jit(solution)/shard_map/all_to_all | solution.py:368
  115.6 1.5 multiply_subtract_fusion
  117.1 19.0 %all_gather.11.rhs_ref = f32[1024,128]{1,0:T(8,128)} all-gather(f32[64,128]{1,0:T(8,128)S(1)} %multiply_subtract_fusion), channel_id=1, replica_groups=mesh['row'=32,'col'=16] {'col'}, dimensions={0}, use_global_device_ids=true | all-gather | bytes 557056 | tf_op jit(solution)/shard_map/all_gather | solution.py:374
  136.1 2.8 %all-gather.3.cloned.1.call-done.a_ref = f32[1024,1024]{1,0:T(8,128)} async-done(((f32[64,1024]{1,0:T(8,128)}), f32[1024,1024]{1,0:T(8,128)}) %all-gather.3.cloned.1.call-update) | async-done | bytes 4194320 | tf_op jit(solution)/shard_map/all_gather | solution.py:362
  138.9 35.4 %shard_map.98 = (f32[64,1024]{1,0:T(8,128)}, f32[64,64]{1,0:T(8,128)}, f32[64,64]{1,0:T(8,128)}) custom-call(s32[1]{0:T(128)} %bitcast.c_ref, f32[1024,1024]{1,0:T(8,128)} %all-gather.3.cloned.1.call-done.a_ref, f32[1024,128]{1,0:T(8,128)} %all_gather.11.rhs_ref), custom_call_target="tpu_custom_call" | custom-call | flops 3000000000 | bytes 5000000 | tf_op jit(solution)/shard_map/pallas_call | solution.py:177
  (35 shorter events, 1.1 us)
Async XLA Ops:
  7.2 0.8 copy-start
  7.9 0.7 copy-start.1
  8.6 14.9 %copy-start.6 = (f32[32]{0:T(128)S(1)}, f32[32]{0:T(128)}, u32[]{:S(2)}) copy-start(f32[32]{0:T(128)} %param.13) | copy-start | bytes 388
  8.6 16.2 %copy-start.4 = (bf16[64,160]{1,0:T(8,128)(2,1)S(1)}, bf16[64,160]{1,0:T(8,128)(2,1)}, u32[]{:S(2)}) copy-start(bf16[64,160]{1,0:T(8,128)(2,1)} %param.7) | copy-start | bytes 61444
  8.6 16.3 %copy-start.5 = (bf16[64,160]{1,0:T(8,128)(2,1)S(1)}, bf16[64,160]{1,0:T(8,128)(2,1)}, u32[]{:S(2)}) copy-start(bf16[64,160]{1,0:T(8,128)(2,1)} %param.9) | copy-start | bytes 61444
  9.7 34.1 %all-to-all-start = ((bf16[32,104,128]{2,1,0:T(8,128)(2,1)}), bf16[32,104,128]{2,1,0:T(8,128)(2,1)S(1)}, u32[]{:S(2)}, u32[]{:S(2)}) async-start(bf16[32,104,128]{2,1,0:T(8,128)(2,1)} %shard_map.94), calls=%async_computation | async-start | bytes 1703936 | tf_op jit(solution)/shard_map/all_to_all | solution.py:335
  23.5 78.5 %all-gather.5.cloned.1.call-start = ((), (), s32[]{:S(2)}) async-start(), calls=%async_computation.5 | async-start | bytes 1392640 | tf_op jit(solution)/shard_map/all_gather | solution.py:332
  23.5 36.5 %collective-permute-start.1 = (f32[32]{0:T(128)S(1)}, f32[32]{0:T(128)S(1)}, u32[]{:S(2)}, u32[]{:S(2)}) collective-permute-start(f32[32]{0:T(128)S(1)} %copy-done.6), channel_id=1, source_target_pairs={{0,0},{16,16},{33,1},{49,17},{66,2},{82,18},{99,3},{115,19},{132,4... | collective-permute-start | bytes 392 | tf_op jit(solution)/shard_map/ppermute | solution.py:337
  45.8 13.5 %collective-permute-start = (bf16[640,128]{1,0:T(8,128)(2,1)S(1)}, bf16[640,128]{1,0:T(8,128)(2,1)S(1)}, u32[]{:S(2)}, u32[]{:S(2)}) collective-permute-start(bf16[640,128]{1,0:T(8,128)(2,1)S(1)} %get-tuple-element.8), channel_id=1, source_target_pairs={{0,0},{1,1},{2,2},{3,3},{4,4},{5,5},{6,6},{7,7},{8,8},{9,9},{10,10... | collective-permute-start | bytes 491528 | tf_op jit(solution)/shard_map/ppermute | solution.py:345
  46.5 21.7 %all-to-all-start.1 = ((f32[16,16,128]{2,1,0:T(8,128)}), f32[16,16,128]{2,1,0:T(8,128)S(1)}, u32[]{:S(2)}, u32[]{:S(2)}) async-start(f32[16,16,128]{2,1,0:T(8,128)} %get-tuple-element.7), calls=%async_computation.1 | async-start | bytes 262144 | tf_op jit(solution)/shard_map/all_to_all | solution.py:346
  69.0 20.3 %all-to-all-start.2 = ((f32[32,16,128]{2,1,0:T(8,128)}), f32[32,16,128]{2,1,0:T(8,128)S(1)}, u32[]{:S(2)}, u32[]{:S(2)}) async-start(f32[32,16,128]{2,1,0:T(8,128)} %shard_map.96), calls=%async_computation.2 | async-start | bytes 524288 | tf_op jit(solution)/shard_map/all_to_all | solution.py:360
  79.6 59.4 %all-gather.3.cloned.1.call-start = ((), (), s32[]{:S(2)}) async-start(), calls=%async_computation.4 | async-start | bytes 4456448 | tf_op jit(solution)/shard_map/all_gather | solution.py:362
  90.2 0.8 copy-start.2
  90.3 1.1 copy-start.3
  92.5 23.0 %all-to-all-start.3 = ((bf16[16,64,128]{2,1,0:T(8,128)(2,1)}), bf16[16,64,128]{2,1,0:T(8,128)(2,1)S(1)}, u32[]{:S(2)}, u32[]{:S(2)}) async-start(bf16[16,64,128]{2,1,0:T(8,128)(2,1)} %pad_maximum_fusion.2), calls=%async_computation.3 | async-start | bytes 524288 | tf_op jit(solution)/shard_map/all_to_all | solution.py:368
Sparse Core Ops, SparseCore 0:
  26.4 43.5 all-gather.4
  90.4 48.4 all-gather.2
